TPU v7x, 256 devices: a whole 4x4x8 slice. The times are simulated.
256 devices in a mesh: pair: 32 (over z, y), virt: 8 (over x, core).
Axes of the slice: x: 4, y: 4, z: 8, core: 2. Of those that a mesh axis runs over, the one named last changes fastest.
Arguments:
- amplitudes: bfloat16 [16384, 9216], P('pair', 'virt'), may hold values from -6 to 6
- block_mask: int32 [16384, 4], P('pair'), may hold values from 0 to 1, as said below
- integrals: bfloat16 [9216, 9216], P('pair', 'virt'), may hold values from -0.0625 to 0.0625
- mirror: int32 [16384], P('pair'), may hold values from 0 to 16383, as said below
Outputs:
- residual: bfloat16 [16384, 9216], P('pair', 'virt')
Inputs may be any that keep to these rules, and one draw needn't show every extreme that they name: mirror is an involution without fixed points; the pair at local row d * 16 + s of pair index p has its mirror on pair index d, at a local row from p * (16) to p * 16 + 512 // 32 - 1. block_mask[g, 2 * t + u] equals block_mask[mirror[g], 2 * u + t]; every pair has at least one active tile pair.
All inputs are finite; a program needn't handle non-finite values.
Results may differ from a plain program's by a relative error of at most 0.0051.
Values may be sent and summed in bfloat16 or wider, within the bound.
No kernel may reach another device: no remote copies, remote signals or barrier semaphores. Data moves between devices by JAX's collectives and lax.ppermute only.
A program may use at most 192 MiB of HBM per device.

v0:
```python
import jax
import jax.numpy as jnp
from jax import lax
from jax.experimental import pallas as pl
from jax.experimental.pallas import tpu as pltpu
from jax.sharding import Mesh, PartitionSpec as P

TW = 48
V = 96
SIZE = {"z": 8, "y": 4, "x": 4, "c": 2}
NZ, NY, NX = 8, 4, 4
VIRT = 8
PAIR = 32
A_BLOCK = V // VIRT
ROWS = 512
WIDTH = A_BLOCK * V
DEPTH = 288
SLOT = ROWS // PAIR
PLANE = NZ * SLOT
PIECE = A_BLOCK * A_BLOCK
HALF = ROWS // 2
F32 = jnp.float32
BF16 = jnp.bfloat16
ROOM = pltpu.CompilerParams(vmem_limit_bytes=48 * 2**20)


def move(array, axis, by):
    n = SIZE[axis]
    return lax.ppermute(array, axis, [(i, (i + by) % n) for i in range(n)])


def product_kernel(outs_of, where_ref, *refs):
    blocks, b_ref, outs, a_ref = refs[:VIRT], refs[VIRT], refs[VIRT + 1:-1], refs[-1]
    for k, block in enumerate(blocks):
        a_ref[pl.ds(pl.multiple_of(where_ref[k] * DEPTH, 16), DEPTH), :] = block[0]
    value = lax.dot_general(a_ref[...], b_ref[...], (((0,), (0,)), ((), ())), preferred_element_type=F32)
    for g in range(len(outs) // outs_of):
        @pl.when(pl.program_id(0) == g)
        def _():
            rows = ROWS // outs_of
            for h in range(outs_of):
                out = outs[g * outs_of + h]
                out[...] = value[h * rows:(h + 1) * rows, :].astype(out.dtype)


def product(where, group, count, blocks, b, outs_of, kind, *first):
    shape = (ROWS // outs_of, WIDTH)
    whole = pl.BlockSpec((1, DEPTH, ROWS), lambda g, w: (group + g, 0, 0))
    part = pl.BlockSpec((1, DEPTH, ROWS), lambda g, w: (group % (NY // 2) + g, 0, 0))

    def kernel(*refs):
        product_kernel(outs_of, *refs[:VIRT + 2], *refs[VIRT + 2 + len(first):])

    return pl.pallas_call(
        kernel,
        grid_spec=pltpu.PrefetchScalarGridSpec(
            num_scalar_prefetch=1,
            grid=(count,),
            in_specs=[whole] * (VIRT - 2) + [part] * 2 + [pl.BlockSpec((VIRT * DEPTH, WIDTH), lambda g, w: (0, 0))]
            + [pl.BlockSpec(memory_space=pl.ANY)] * len(first),
            out_specs=[pl.BlockSpec(shape, lambda g, w: (0, 0))] * (count * outs_of),
            scratch_shapes=[pltpu.VMEM((VIRT * DEPTH, ROWS), BF16)],
        ),
        out_shape=[jax.ShapeDtypeStruct(shape, kind)] * (count * outs_of),
        compiler_params=ROOM,
    )(where, *blocks, b, *first)


def gather_x(block):
    half = NY // 2
    left = move(block, "x", 1)
    right = move(block, "x", -1)
    far_low = move(left[:half], "x", 1)
    far_high = move(right[half:], "x", -1)
    return [b for one in (block, left, right, far_low, far_high) for b in (one, move(one, "c", 1))]


def joined(near, far):
    return (near.astype(F32) + far.astype(F32)).astype(BF16)


def total_kernel(own_ref, *refs):
    got, out_ref = refs[:4], refs[4]
    for h in range(2):
        rows = slice(h * HALF, (h + 1) * HALF)
        out_ref[rows, :] = (own_ref[rows, :] + got[h][...].astype(F32) + got[2 + h][...].astype(F32)).astype(BF16)


def total(own, *got):
    vmem = pl.BlockSpec(memory_space=pltpu.VMEM)
    return pl.pallas_call(
        total_kernel,
        in_specs=[vmem] * 5,
        out_specs=vmem,
        out_shape=jax.ShapeDtypeStruct((ROWS, WIDTH), BF16),
        compiler_params=ROOM,
    )(own, *got)


def turn_kernel(pick_ref, send_ref, received_ref, *outs):
    picked = jnp.dot(pick_ref[...], received_ref[...], preferred_element_type=F32).astype(BF16)
    turned = lax.dot_general(send_ref[...], picked, (((1,), (1,)), ((), ())), preferred_element_type=F32).astype(BF16)
    for d, out in enumerate(outs):
        for core in range(2):
            out[core] = turned[(2 * d + core) * PIECE:(2 * d + core + 1) * PIECE, :]


def turn(pick, send, received):
    vmem = pl.BlockSpec(memory_space=pltpu.VMEM)
    return pl.pallas_call(
        turn_kernel,
        in_specs=[vmem] * 3,
        out_specs=[vmem] * NX,
        out_shape=[jax.ShapeDtypeStruct((2, PIECE, ROWS), BF16)] * NX,
        compiler_params=ROOM,
    )(pick, send, received)


def finish_kernel(active_ref, land_ref, direct_ref, *refs):
    blocks, across, o_ref, u_ref = refs[:NX], *refs[NX:]
    for k, block in enumerate(blocks):
        u_ref[2 * k * PIECE:(2 * k + 1) * PIECE, :] = block[0]
        u_ref[(2 * k + 1) * PIECE:(2 * k + 2) * PIECE, :] = across[k]
    mirrored = lax.dot_general(u_ref[...], land_ref[...], (((0,), (0,)), ((), ())), preferred_element_type=F32)
    value = direct_ref[...].astype(F32) + mirrored
    column = lax.broadcasted_iota(jnp.int32, (ROWS, WIDTH), 1)
    live = jnp.where(lax.rem(column, V) < TW, active_ref[:, :1], active_ref[:, 1:]) > 0
    o_ref[...] = jnp.where(live, value, 0).astype(BF16)


def finish(active, land, direct, blocks, across):
    vmem = pl.BlockSpec(memory_space=pltpu.VMEM)
    return pl.pallas_call(
        finish_kernel,
        in_specs=[vmem] * (4 + NX),
        out_specs=vmem,
        out_shape=jax.ShapeDtypeStruct((ROWS, WIDTH), BF16),
        scratch_shapes=[pltpu.VMEM((WIDTH, ROWS), BF16)],
        compiler_params=ROOM,
    )(active, land, direct, *blocks, across)


def local(amplitudes, block_mask, integrals, mirror):
    z, y, x, c = (lax.axis_index(n) for n in "zyxc")
    pair = z * NY + y
    tile = (x * 2 + c) * A_BLOCK // TW
    active = lax.dynamic_slice(block_mask, (0, 2 * tile), (ROWS, 2))
    column = jnp.arange(WIDTH, dtype=jnp.int32)
    live = jnp.where(((column % V) < TW)[None, :], active[:, :1], active[:, 1:]) > 0

    whole = lax.all_gather(integrals, "z", axis=0, tiled=True)

    masked = jnp.where(live, amplitudes, jnp.zeros_like(amplitudes))
    turned = masked.T.reshape(NY, DEPTH, ROWS)

    def toward(d):
        return lax.dynamic_slice_in_dim(turned, (y + d) % NY, 1, axis=0)

    groups = [toward(0), move(toward(2), "y", 2), move(toward(-1), "y", -1), move(toward(1), "y", 1)]
    blocks = gather_x(jnp.concatenate(groups, axis=0))
    low, high = blocks[:VIRT], blocks[:VIRT - 2] + blocks[VIRT:]
    where = jnp.stack([(x + d) % NX * 2 + core for d in (0, -1, 1, 2) for core in (c, 1 - c)]).astype(jnp.int32)

    far_low, far_high = product(where, 1, 1, low, whole, 2, BF16)
    from_down = move(far_low, "y", 1)
    from_up = move(far_high, "y", -1)
    up_low, up_high, down_low, down_high = product(where, 2, 2, high, whole, 2, BF16, far_low)
    from_down_high = move(up_high, "y", 1)
    from_up_low = move(down_low, "y", -1)
    up_low, down_high = joined(up_low, from_down), joined(down_high, from_up)
    from_down_low = move(up_low, "y", 1)
    from_up_high = move(down_high, "y", -1)
    own, = product(where, 0, 1, low, whole, 1, F32, up_low, down_high)
    direct = total(own, from_down_low, from_down_high, from_up_low, from_up_high)

    source = mirror // ROWS
    position = source * SLOT + mirror % ROWS - pair * SLOT
    row = jnp.arange(ROWS, dtype=jnp.int32)
    pick = (position[:, None] == row[None, :]).astype(BF16)
    core, step, second, first = column // PIECE % 2, column // (2 * PIECE), column % PIECE // A_BLOCK, column % A_BLOCK
    target = (x + step) % NX * 2 + (c + core) % 2
    send = ((first * V + target * A_BLOCK + second)[:, None] == column[None, :]).astype(BF16)
    origin = (x + NX - step) % NX * 2 + (c + core) % 2
    land = ((second * V + origin * A_BLOCK + first)[:, None] == column[None, :]).astype(BF16)

    received = lax.all_to_all(direct.reshape(PAIR, SLOT, WIDTH), ("z", "y"), split_axis=0, concat_axis=0, tiled=True)
    sent = turn(pick, send, received.reshape(ROWS, WIDTH))
    arrived = [sent[0]] + [move(sent[d], "x", d) for d in range(1, NX)]
    across = move(jnp.concatenate([block[1:] for block in arrived], axis=0), "c", 1)
    return finish(active, land, direct, arrived, across)


def solution(mesh):
    grid = Mesh(mesh.devices.reshape(tuple(SIZE.values())), tuple(SIZE))
    rows, columns = ("z", "y"), ("x", "c")
    in_specs = (P(rows, columns), P(rows, None), P(rows, columns), P(rows))
    return jax.shard_map(local, mesh=grid, in_specs=in_specs, out_specs=P(rows, columns), check_vma=False)
```

profile of v0, /device:TPU:8, one launch (start us, length us, event | category | flops | bytes accessed | tf_op | source)
XLA Modules:
  0.0 203.4 jit_solution(8478857280217730979)
XLA Ops:
  9.4 2.4 %collective-permute-start = (bf16[1,288,512]{2,1,0:T(8,128)(2,1)S(1)}, bf16[1,288,512]{2,1,0:T(8,128)(2,1)S(1)}, u32[]{:S(2)}, u32[]{:S(2)}) collective-permute-start(bf16[1,288,512]{2,1,0:T(8,128)(2,1)S(1)} %get-tuple-element.30), channel_id=1, source_target_pairs={{0,16},{8,24},{16,0},{24,8},{1,17},{9,25},{17,1},{25,9},{2,18},{10... | collective-permute-start | bytes 884744 | tf_op jit(solution)/shard_map/ppermute | solution.py:29
  11.8 1.3 collective-permute-start.1
  13.8 7.1 %collective-permute-done = bf16[1,288,512]{2,1,0:T(8,128)(2,1)S(1)} collective-permute-done((bf16[1,288,512]{2,1,0:T(8,128)(2,1)S(1)}, bf16[1,288,512]{2,1,0:T(8,128)(2,1)S(1)}, u32[]{:S(2)}, u32[]{:S(2)}) %collective-permute-start) | collective-permute-done | bytes 294944 | tf_op jit(solution)/shard_map/ppermute | solution.py:29
  20.9 5.1 %collective-permute-done.1 = bf16[1,288,512]{2,1,0:T(8,128)(2,1)S(1)} collective-permute-done((bf16[1,288,512]{2,1,0:T(8,128)(2,1)S(1)}, bf16[1,288,512]{2,1,0:T(8,128)(2,1)S(1)}, u32[]{:S(2)}, u32[]{:S(2)}) %collective-permute-start.1) | collective-permute-done | bytes 294944 | tf_op jit(solution)/shard_map/ppermute | solution.py:29
  26.3 1.6 collective-permute-start.4
  27.9 1.7 collective-permute-start.6
  29.7 25.8 %collective-permute-done.4.refs_3_ = bf16[4,288,512]{2,1,0:T(8,128)(2,1)S(1)} collective-permute-done((bf16[4,288,512]{2,1,0:T(8,128)(2,1)S(1)}, bf16[4,288,512]{2,1,0:T(8,128)(2,1)S(1)}, u32[]{:S(2)}, u32[]{:S(2)}) %collective-permute-start.4) | collective-permute-done | bytes 1179680 | tf_op jit(solution)/shard_map/ppermute | solution.py:29
  56.4 1.9 slice.35
  58.3 3.0 %collective-permute-start.10 = (bf16[2,288,512]{2,1,0:T(8,128)(2,1)}, bf16[2,288,512]{2,1,0:T(8,128)(2,1)}, u32[]{:S(2)}, u32[]{:S(2)}) collective-permute-start(bf16[2,288,512]{2,1,0:T(8,128)(2,1)} %slice.35), channel_id=1, source_target_pairs={{0,6},{2,0},{4,2},{6,4},{1,7},{3,1},{5,3},{7,5},{8,14},{10,8},{12,... | collective-permute-start | bytes 1769480 | tf_op jit(solution)/shard_map/ppermute | solution.py:29
  61.3 10.1 %collective-permute-done.8.refs_7_ = bf16[2,288,512]{2,1,0:T(8,128)(2,1)} collective-permute-done((bf16[2,288,512]{2,1,0:T(8,128)(2,1)S(1)}, bf16[2,288,512]{2,1,0:T(8,128)(2,1)}, u32[]{:S(2)}, u32[]{:S(2)}) %collective-permute-start.8) | collective-permute-done | bytes 589856 | tf_op jit(solution)/shard_map/ppermute | solution.py:29
  71.4 2.9 %collective-permute-done.10.refs_7_ = bf16[2,288,512]{2,1,0:T(8,128)(2,1)} collective-permute-done((bf16[2,288,512]{2,1,0:T(8,128)(2,1)}, bf16[2,288,512]{2,1,0:T(8,128)(2,1)}, u32[]{:S(2)}, u32[]{:S(2)}) %collective-permute-start.10) | collective-permute-done | bytes 589856 | tf_op jit(solution)/shard_map/ppermute | solution.py:29
  74.4 3.0 %all-gather.2.cloned.1.call-done.refs_9_ = bf16[2304,1152]{1,0:T(8,128)(2,1)} async-done(((bf16[288,1152]{1,0:T(8,128)(2,1)}), bf16[2304,1152]{1,0:T(8,128)(2,1)}) %all-gather.2.cloned.1.call-update) | async-done | bytes 5308432 | tf_op jit(solution)/shard_map/all_gather | solution.py:151
  77.3 6.9 %shard_map.46 = (bf16[256,1152]{1,0:T(8,128)(2,1)S(1)}, bf16[256,1152]{1,0:T(8,128)(2,1)S(1)}) custom-call(s32[8]{0:T(128)S(1)} %stack.35.refs_0_, bf16[4,288,512]{2,1,0:T(8,128)(2,1)S(1)} %pad_maximum_fusion.refs_1_, bf16[4,288,512]{2,1,0:T(8,128)(2,1)S(1)} %collective-permute-done.3.refs_2_, bf16[4,288,512]{2,1,0:T(8,128)(2,1)S(1)} %collective-permute-done.4.refs_3_, ...), custom_call_target="tpu_custom_call" | custom-call | tf_op jit(solution)/shard_map/pallas_call | solution.py:54
  84.9 1.5 collective-permute-start.12
  86.4 11.1 %shard_map.47 = (bf16[256,1152]{1,0:T(8,128)(2,1)S(1)}, bf16[256,1152]{1,0:T(8,128)(2,1)S(1)}, bf16[256,1152]{1,0:T(8,128)(2,1)S(1)}, bf16[256,1152]{1,0:T(8,128)(2,1)S(1)}) custom-call(s32[8]{0:T(128)S(1)} %stack.35.refs_0_, bf16[4,288,512]{2,1,0:T(8,128)(2,1)S(1)} %pad_maximum_fusion.refs_1_, bf16[4,288,512]{2,1,0:T(8,128)(2,1)} %copy-done.3, ...), custom_call_target="tpu_custom_call" | custom-call | tf_op jit(solution)/shard_map/pallas_call | solution.py:54
  97.5 1.6 collective-permute-start.15
  99.8 2.6 %collective-permute-start.17 = (bf16[256,1152]{1,0:T(8,128)(2,1)S(1)}, bf16[256,1152]{1,0:T(8,128)(2,1)S(1)}, u32[]{:S(2)}, u32[]{:S(2)}) collective-permute-start(bf16[256,1152]{1,0:T(8,128)(2,1)S(1)} %add_convert_fusion.refs_11_), channel_id=1, source_target_pairs={{0,24},{8,0},{16,8},{24,16},{1,25},{9,1},{17,9},{25,17},{2,26},{10... | collective-permute-start | bytes 1769480 | tf_op jit(solution)/shard_map/ppermute | solution.py:29
  102.9 8.3 %shard_map.48.own_ref = f32[512,1152]{1,0:T(8,128)} custom-call(s32[8]{0:T(128)S(1)} %stack.35.refs_0_, bf16[4,288,512]{2,1,0:T(8,128)(2,1)S(1)} %pad_maximum_fusion.refs_1_, bf16[4,288,512]{2,1,0:T(8,128)(2,1)S(1)} %copy-done.4, bf16[4,288,512]{2,1,0:T(8,128)(2,1)S(1)} %copy-done.2, bf16[4,288,512]{2,1,0:T(8,128)(2,1)} %collective-permute-done.5.refs_4_, ...), custom_call_target="tpu_custom_call" | custom-call | tf_op jit(solution)/shard_map/pallas_call | solution.py:54
  111.2 3.2 %collective-permute-done.15.refs_1_ = bf16[256,1152]{1,0:T(8,128)(2,1)S(1)} collective-permute-done((bf16[256,1152]{1,0:T(8,128)(2,1)S(1)}, bf16[256,1152]{1,0:T(8,128)(2,1)S(1)}, u32[]{:S(2)}, u32[]{:S(2)}) %collective-permute-start.15) | collective-permute-done | bytes 589856 | tf_op jit(solution)/shard_map/ppermute | solution.py:29
  114.5 1.3 collective-permute-done.16.refs_2_
  115.7 10.9 %collective-permute-done.17.refs_3_ = bf16[256,1152]{1,0:T(8,128)(2,1)S(1)} collective-permute-done((bf16[256,1152]{1,0:T(8,128)(2,1)S(1)}, bf16[256,1152]{1,0:T(8,128)(2,1)S(1)}, u32[]{:S(2)}, u32[]{:S(2)}) %collective-permute-start.17) | collective-permute-done | bytes 589856 | tf_op jit(solution)/shard_map/ppermute | solution.py:29
  126.6 1.7 copy-done.5
  128.3 1.4 shard_map.49.direct_ref
  129.6 10.1 %all-to-all-start = ((bf16[32,16,1152]{2,1,0:T(8,128)(2,1)}), bf16[32,16,1152]{2,1,0:T(8,128)(2,1)}, u32[]{:S(2)}, u32[]{:S(2)}) async-start(bf16[32,16,1152]{2,1,0:T(8,128)(2,1)} %bitcast.10), calls=%async_computation | async-start | bytes 2359296 | tf_op jit(solution)/shard_map/all_to_all | solution.py:186
  140.5 29.4 %all-to-all-done = bf16[32,16,1152]{2,1,0:T(8,128)(2,1)} async-done(((bf16[32,16,1152]{2,1,0:T(8,128)(2,1)}), bf16[32,16,1152]{2,1,0:T(8,128)(2,1)}, u32[]{:S(2)}, u32[]{:S(2)}) %all-to-all-start) | async-done | bytes 1179680 | tf_op jit(solution)/shard_map/all_to_all | solution.py:186
  169.9 4.4 %shard_map.50 = (bf16[2,144,512]{2,1,0:T(8,128)(2,1)S(1)}, bf16[2,144,512]{2,1,0:T(8,128)(2,1)}, bf16[2,144,512]{2,1,0:T(8,128)(2,1)}, bf16[2,144,512]{2,1,0:T(8,128)(2,1)}) custom-call(bf16[512,512]{1,0:T(8,128)(2,1)S(1)} %fusion.4.pick_ref, bf16[1152,1152]{1,0:T(8,128)(2,1)S(1)} %fusion.1.send_ref, bf16[512,1152]{1,0:T(8,128)(2,1)} %bitcast.11.received_ref), custom_call_target="tpu_custom_call" | custom-call | tf_op jit(solution)/shard_map/pallas_call | solution.py:110
  174.4 1.0 collective-permute-start.18
  175.4 4.1 %collective-permute-start.19 = (bf16[2,144,512]{2,1,0:T(8,128)(2,1)}, bf16[2,144,512]{2,1,0:T(8,128)(2,1)S(1)}, u32[]{:S(2)}, u32[]{:S(2)}) collective-permute-start(bf16[2,144,512]{2,1,0:T(8,128)(2,1)} %get-tuple-element.23), channel_id=1, source_target_pairs={{0,4},{2,6},{4,0},{6,2},{1,5},{3,7},{5,1},{7,3},{8,12},{10,14},{12... | collective-permute-start | bytes 884744 | tf_op jit(solution)/shard_map/ppermute | solution.py:29
  179.6 6.2 %collective-permute-done.18.refs_1_ = bf16[2,144,512]{2,1,0:T(8,128)(2,1)S(1)} collective-permute-done((bf16[2,144,512]{2,1,0:T(8,128)(2,1)}, bf16[2,144,512]{2,1,0:T(8,128)(2,1)S(1)}, u32[]{:S(2)}, u32[]{:S(2)}) %collective-permute-start.18) | collective-permute-done | bytes 294944 | tf_op jit(solution)/shard_map/ppermute | solution.py:29
  185.8 4.4 %collective-permute-done.19.refs_2_ = bf16[2,144,512]{2,1,0:T(8,128)(2,1)S(1)} collective-permute-done((bf16[2,144,512]{2,1,0:T(8,128)(2,1)}, bf16[2,144,512]{2,1,0:T(8,128)(2,1)S(1)}, u32[]{:S(2)}, u32[]{:S(2)}) %collective-permute-start.19) | collective-permute-done | bytes 294944 | tf_op jit(solution)/shard_map/ppermute | solution.py:29
  191.0 1.5 collective-permute-done.21.refs_4_
  192.4 4.2 %shard_map.51 = bf16[512,1152]{1,0:T(8,128)(2,1)} custom-call(s32[512,2]{1,0:T(8,128)S(1)} %copy-done.7, bf16[1152,1152]{1,0:T(8,128)(2,1)S(1)} %fusion.land_ref, bf16[512,1152]{1,0:T(8,128)(2,1)} %shard_map.49.direct_ref, bf16[2,144,512]{2,1,0:T(8,128)(2,1)S(1)} %get-tuple-element.21.refs_0_, bf16[2,144,512]{2,1,0:T(8,128)(2,1)S(1)} %collective-permute-done.18.refs_1_, ...), custom_call_target="tpu_custom_call" | custom-call | tf_op jit(solution)/shard_map/pallas_call | solution.py:133
  (67 shorter events, 7.9 us)
Async XLA Ops:
  6.5 1.3 copy-start.8
  6.5 70.8 %all-gather.2.cloned.1.call-start = ((), (), s32[]{:S(2)}) async-start(), calls=%async_computation.1 | async-start | bytes 5971968 | tf_op jit(solution)/shard_map/all_gather | solution.py:151
  9.4 11.5 %collective-permute-start = (bf16[1,288,512]{2,1,0:T(8,128)(2,1)S(1)}, bf16[1,288,512]{2,1,0:T(8,128)(2,1)S(1)}, u32[]{:S(2)}, u32[]{:S(2)}) collective-permute-start(bf16[1,288,512]{2,1,0:T(8,128)(2,1)S(1)} %get-tuple-element.30), channel_id=1, source_target_pairs={{0,16},{8,24},{16,0},{24,8},{1,17},{9,25},{17,1},{25,9},{2,18},{10... | collective-permute-start | bytes 884744 | tf_op jit(solution)/shard_map/ppermute | solution.py:29
  11.8 14.3 %collective-permute-start.1 = (bf16[1,288,512]{2,1,0:T(8,128)(2,1)S(1)}, bf16[1,288,512]{2,1,0:T(8,128)(2,1)S(1)}, u32[]{:S(2)}, u32[]{:S(2)}) collective-permute-start(bf16[1,288,512]{2,1,0:T(8,128)(2,1)S(1)} %get-tuple-element.29), channel_id=1, source_target_pairs={{0,24},{8,0},{16,8},{24,16},{1,25},{9,1},{17,9},{25,17},{2,26},{10... | collective-permute-start | bytes 884744 | tf_op jit(solution)/shard_map/ppermute | solution.py:29
  13.1 13.1 %collective-permute-start.2 = (bf16[1,288,512]{2,1,0:T(8,128)(2,1)S(1)}, bf16[1,288,512]{2,1,0:T(8,128)(2,1)S(1)}, u32[]{:S(2)}, u32[]{:S(2)}) collective-permute-start(bf16[1,288,512]{2,1,0:T(8,128)(2,1)S(1)} %get-tuple-element.28), channel_id=1, source_target_pairs={{0,8},{8,16},{16,24},{24,0},{1,9},{9,17},{17,25},{25,1},{2,10},{10... | collective-permute-start | bytes 884744 | tf_op jit(solution)/shard_map/ppermute | solution.py:29
  26.3 29.1 %collective-permute-start.4 = (bf16[4,288,512]{2,1,0:T(8,128)(2,1)S(1)}, bf16[4,288,512]{2,1,0:T(8,128)(2,1)S(1)}, u32[]{:S(2)}, u32[]{:S(2)}) collective-permute-start(bf16[4,288,512]{2,1,0:T(8,128)(2,1)S(1)} %pad_maximum_fusion.refs_1_), channel_id=1, source_target_pairs={{0,2},{2,4},{4,6},{6,0},{1,3},{3,5},{5,7},{7,1},{8,10},{10,12},{12... | collective-permute-start | bytes 3538952 | tf_op jit(solution)/shard_map/ppermute | solution.py:29
  27.9 28.0 %collective-permute-start.6 = (bf16[4,288,512]{2,1,0:T(8,128)(2,1)S(1)}, bf16[4,288,512]{2,1,0:T(8,128)(2,1)}, u32[]{:S(2)}, u32[]{:S(2)}) collective-permute-start(bf16[4,288,512]{2,1,0:T(8,128)(2,1)S(1)} %pad_maximum_fusion.refs_1_), channel_id=1, source_target_pairs={{0,6},{2,0},{4,2},{6,4},{1,7},{3,1},{5,3},{7,5},{8,14},{10,8},{12,... | collective-permute-start | bytes 3538952 | tf_op jit(solution)/shard_map/ppermute | solution.py:29
  29.7 44.7 %collective-permute-start.3 = (bf16[4,288,512]{2,1,0:T(8,128)(2,1)S(1)}, bf16[4,288,512]{2,1,0:T(8,128)(2,1)S(1)}, u32[]{:S(2)}, u32[]{:S(2)}) collective-permute-start(bf16[4,288,512]{2,1,0:T(8,128)(2,1)S(1)} %pad_maximum_fusion.refs_1_), channel_id=1, source_target_pairs={{0,1},{1,0},{2,3},{3,2},{4,5},{5,4},{6,7},{7,6},{8,9},{9,8},{10,11... | collective-permute-start | bytes 3538952 | tf_op jit(solution)/shard_map/ppermute | solution.py:29
  55.5 21.9 %copy-start.1 = (bf16[4,288,512]{2,1,0:T(8,128)(2,1)}, bf16[4,288,512]{2,1,0:T(8,128)(2,1)S(1)}, u32[]{:S(2)}) copy-start(bf16[4,288,512]{2,1,0:T(8,128)(2,1)S(1)} %collective-permute-done.4.refs_3_) | copy-start | bytes 3538948
  55.5 15.8 %collective-permute-start.8 = (bf16[2,288,512]{2,1,0:T(8,128)(2,1)S(1)}, bf16[2,288,512]{2,1,0:T(8,128)(2,1)}, u32[]{:S(2)}, u32[]{:S(2)}) collective-permute-start(bf16[2,288,512]{2,1,0:T(8,128)(2,1)S(1)} %slice.34), channel_id=1, source_target_pairs={{0,2},{2,4},{4,6},{6,0},{1,3},{3,5},{5,7},{7,1},{8,10},{10,12},{12... | collective-permute-start | bytes 1769480 | tf_op jit(solution)/shard_map/ppermute | solution.py:29
  55.9 18.5 %collective-permute-start.5 = (bf16[4,288,512]{2,1,0:T(8,128)(2,1)S(1)}, bf16[4,288,512]{2,1,0:T(8,128)(2,1)}, u32[]{:S(2)}, u32[]{:S(2)}) collective-permute-start(bf16[4,288,512]{2,1,0:T(8,128)(2,1)S(1)} %collective-permute-done.4.refs_3_), channel_id=1, source_target_pairs={{0,1},{1,0},{2,3},{3,2},{4,5},{5,4},{6,7},{7,6},{8,9},{9,8},{10,11... | collective-permute-start | bytes 3538952 | tf_op jit(solution)/shard_map/ppermute | solution.py:29
  55.9 18.5 %collective-permute-start.7 = (bf16[4,288,512]{2,1,0:T(8,128)(2,1)}, bf16[4,288,512]{2,1,0:T(8,128)(2,1)}, u32[]{:S(2)}, u32[]{:S(2)}) collective-permute-start(bf16[4,288,512]{2,1,0:T(8,128)(2,1)} %collective-permute-done.6.refs_5_), channel_id=1, source_target_pairs={{0,1},{1,0},{2,3},{3,2},{4,5},{5,4},{6,7},{7,6},{8,9},{9,8},{10,11... | collective-permute-start | bytes 3538952 | tf_op jit(solution)/shard_map/ppermute | solution.py:29
  58.3 16.0 %collective-permute-start.10 = (bf16[2,288,512]{2,1,0:T(8,128)(2,1)}, bf16[2,288,512]{2,1,0:T(8,128)(2,1)}, u32[]{:S(2)}, u32[]{:S(2)}) collective-permute-start(bf16[2,288,512]{2,1,0:T(8,128)(2,1)} %slice.35), channel_id=1, source_target_pairs={{0,6},{2,0},{4,2},{6,4},{1,7},{3,1},{5,3},{7,5},{8,14},{10,8},{12,... | collective-permute-start | bytes 1769480 | tf_op jit(solution)/shard_map/ppermute | solution.py:29
  71.4 3.0 %collective-permute-start.9 = (bf16[2,288,512]{2,1,0:T(8,128)(2,1)}, bf16[2,288,512]{2,1,0:T(8,128)(2,1)}, u32[]{:S(2)}, u32[]{:S(2)}) collective-permute-start(bf16[2,288,512]{2,1,0:T(8,128)(2,1)} %collective-permute-done.8.refs_7_), channel_id=1, source_target_pairs={{0,1},{1,0},{2,3},{3,2},{4,5},{5,4},{6,7},{7,6},{8,9},{9,8},{10,11... | collective-permute-start | bytes 1769480 | tf_op jit(solution)/shard_map/ppermute | solution.py:29
  74.3 12.0 %collective-permute-start.11 = (bf16[2,288,512]{2,1,0:T(8,128)(2,1)}, bf16[2,288,512]{2,1,0:T(8,128)(2,1)}, u32[]{:S(2)}, u32[]{:S(2)}) collective-permute-start(bf16[2,288,512]{2,1,0:T(8,128)(2,1)} %collective-permute-done.10.refs_7_), channel_id=1, source_target_pairs={{0,1},{1,0},{2,3},{3,2},{4,5},{5,4},{6,7},{7,6},{8,9},{9,8},{10,11... | collective-permute-start | bytes 1769480 | tf_op jit(solution)/shard_map/ppermute | solution.py:29
  74.3 9.9 %copy-start.3 = (bf16[4,288,512]{2,1,0:T(8,128)(2,1)}, bf16[4,288,512]{2,1,0:T(8,128)(2,1)S(1)}, u32[]{:S(2)}) copy-start(bf16[4,288,512]{2,1,0:T(8,128)(2,1)S(1)} %collective-permute-done.3.refs_2_) | copy-start | bytes 3538948
  84.3 15.3 %collective-permute-start.13 = (bf16[256,1152]{1,0:T(8,128)(2,1)S(1)}, bf16[256,1152]{1,0:T(8,128)(2,1)S(1)}, u32[]{:S(2)}, u32[]{:S(2)}) collective-permute-start(bf16[256,1152]{1,0:T(8,128)(2,1)S(1)} %get-tuple-element.18), channel_id=1, source_target_pairs={{0,24},{8,0},{16,8},{24,16},{1,25},{9,1},{17,9},{25,17},{2,26},{10... | collective-permute-start | bytes 1769480 | tf_op jit(solution)/shard_map/ppermute | solution.py:29
  84.9 17.5 %collective-permute-start.12 = (bf16[256,1152]{1,0:T(8,128)(2,1)S(1)}, bf16[256,1152]{1,0:T(8,128)(2,1)S(1)}, u32[]{:S(2)}, u32[]{:S(2)}) collective-permute-start(bf16[256,1152]{1,0:T(8,128)(2,1)S(1)} %get-tuple-element.15.refs_10_), channel_id=1, source_target_pairs={{0,8},{8,16},{16,24},{24,0},{1,9},{9,17},{17,25},{25,1},{2,10},{10... | collective-permute-start | bytes 1769480 | tf_op jit(solution)/shard_map/ppermute | solution.py:29
  97.5 17.0 %collective-permute-start.15 = (bf16[256,1152]{1,0:T(8,128)(2,1)S(1)}, bf16[256,1152]{1,0:T(8,128)(2,1)S(1)}, u32[]{:S(2)}, u32[]{:S(2)}) collective-permute-start(bf16[256,1152]{1,0:T(8,128)(2,1)S(1)} %get-tuple-element.19), channel_id=1, source_target_pairs={{0,8},{8,16},{16,24},{24,0},{1,9},{9,17},{17,25},{25,1},{2,10},{10... | collective-permute-start | bytes 1769480 | tf_op jit(solution)/shard_map/ppermute | solution.py:29
  99.1 16.6 %collective-permute-start.16 = (bf16[256,1152]{1,0:T(8,128)(2,1)S(1)}, bf16[256,1152]{1,0:T(8,128)(2,1)S(1)}, u32[]{:S(2)}, u32[]{:S(2)}) collective-permute-start(bf16[256,1152]{1,0:T(8,128)(2,1)S(1)} %get-tuple-element.20), channel_id=1, source_target_pairs={{0,24},{8,0},{16,8},{24,16},{1,25},{9,1},{17,9},{25,17},{2,26},{10... | collective-permute-start | bytes 1769480 | tf_op jit(solution)/shard_map/ppermute | solution.py:29
  99.6 3.3 %copy-start.4 = (bf16[4,288,512]{2,1,0:T(8,128)(2,1)S(1)}, bf16[4,288,512]{2,1,0:T(8,128)(2,1)}, u32[]{:S(2)}) copy-start(bf16[4,288,512]{2,1,0:T(8,128)(2,1)} %copy-done.3) | copy-start | bytes 3538948
  99.8 3.1 %copy-start.2 = (bf16[4,288,512]{2,1,0:T(8,128)(2,1)S(1)}, bf16[4,288,512]{2,1,0:T(8,128)(2,1)}, u32[]{:S(2)}) copy-start(bf16[4,288,512]{2,1,0:T(8,128)(2,1)} %copy-done.1) | copy-start | bytes 3538948
  99.8 26.8 %collective-permute-start.17 = (bf16[256,1152]{1,0:T(8,128)(2,1)S(1)}, bf16[256,1152]{1,0:T(8,128)(2,1)S(1)}, u32[]{:S(2)}, u32[]{:S(2)}) collective-permute-start(bf16[256,1152]{1,0:T(8,128)(2,1)S(1)} %add_convert_fusion.refs_11_), channel_id=1, source_target_pairs={{0,24},{8,0},{16,8},{24,16},{1,25},{9,1},{17,9},{25,17},{2,26},{10... | collective-permute-start | bytes 1769480 | tf_op jit(solution)/shard_map/ppermute | solution.py:29
  102.6 24.0 %collective-permute-start.14 = (bf16[256,1152]{1,0:T(8,128)(2,1)S(1)}, bf16[256,1152]{1,0:T(8,128)(2,1)S(1)}, u32[]{:S(2)}, u32[]{:S(2)}) collective-permute-start(bf16[256,1152]{1,0:T(8,128)(2,1)S(1)} %add_convert_fusion.1.refs_10_), channel_id=1, source_target_pairs={{0,8},{8,16},{16,24},{24,0},{1,9},{9,17},{17,25},{25,1},{2,10},{10... | collective-permute-start | bytes 1769480 | tf_op jit(solution)/shard_map/ppermute | solution.py:29
  126.6 1.7 copy-start.5
  129.6 10.2 %copy-start.9 = (s32[512]{0:T(512)S(1)}, s32[512]{0:T(512)}, u32[]{:S(2)}) copy-start(s32[512]{0:T(512)} %param.7) | copy-start | bytes 6148
  129.6 40.3 %all-to-all-start = ((bf16[32,16,1152]{2,1,0:T(8,128)(2,1)}), bf16[32,16,1152]{2,1,0:T(8,128)(2,1)}, u32[]{:S(2)}, u32[]{:S(2)}) async-start(bf16[32,16,1152]{2,1,0:T(8,128)(2,1)} %bitcast.10), calls=%async_computation | async-start | bytes 2359296 | tf_op jit(solution)/shard_map/all_to_all | solution.py:186
  174.4 11.4 %collective-permute-start.18 = (bf16[2,144,512]{2,1,0:T(8,128)(2,1)}, bf16[2,144,512]{2,1,0:T(8,128)(2,1)S(1)}, u32[]{:S(2)}, u32[]{:S(2)}) collective-permute-start(bf16[2,144,512]{2,1,0:T(8,128)(2,1)} %get-tuple-element.22), channel_id=1, source_target_pairs={{0,2},{2,4},{4,6},{6,0},{1,3},{3,5},{5,7},{7,1},{8,10},{10,12},{12... | collective-permute-start | bytes 884744 | tf_op jit(solution)/shard_map/ppermute | solution.py:29
  175.4 14.8 %collective-permute-start.19 = (bf16[2,144,512]{2,1,0:T(8,128)(2,1)}, bf16[2,144,512]{2,1,0:T(8,128)(2,1)S(1)}, u32[]{:S(2)}, u32[]{:S(2)}) collective-permute-start(bf16[2,144,512]{2,1,0:T(8,128)(2,1)} %get-tuple-element.23), channel_id=1, source_target_pairs={{0,4},{2,6},{4,0},{6,2},{1,5},{3,7},{5,1},{7,3},{8,12},{10,14},{12... | collective-permute-start | bytes 884744 | tf_op jit(solution)/shard_map/ppermute | solution.py:29
  179.5 10.7 %collective-permute-start.20 = (bf16[2,144,512]{2,1,0:T(8,128)(2,1)}, bf16[2,144,512]{2,1,0:T(8,128)(2,1)S(1)}, u32[]{:S(2)}, u32[]{:S(2)}) collective-permute-start(bf16[2,144,512]{2,1,0:T(8,128)(2,1)} %get-tuple-element.24), channel_id=1, source_target_pairs={{0,6},{2,0},{4,2},{6,4},{1,7},{3,1},{5,3},{7,5},{8,14},{10,8},{12,... | collective-permute-start | bytes 884744 | tf_op jit(solution)/shard_map/ppermute | solution.py:29
  190.3 2.1 %copy-start.7 = (s32[512,2]{1,0:T(8,128)S(1)}, s32[512,2]{1,0:T(8,128)}, u32[]{:S(2)}) copy-start(s32[512,2]{1,0:T(8,128)} %copy-done.6) | copy-start | bytes 12292
  190.3 2.1 %collective-permute-start.21 = (bf16[4,144,512]{2,1,0:T(8,128)(2,1)S(1)}, bf16[4,144,512]{2,1,0:T(8,128)(2,1)S(1)}, u32[]{:S(2)}, u32[]{:S(2)}) collective-permute-start(bf16[4,144,512]{2,1,0:T(8,128)(2,1)S(1)} %pad_maximum_fusion.1), channel_id=1, source_target_pairs={{0,1},{1,0},{2,3},{3,2},{4,5},{5,4},{6,7},{7,6},{8,9},{9,8},{10,11... | collective-permute-start | bytes 1769480 | tf_op jit(solution)/shard_map/ppermute | solution.py:29
  (2 other events, 1.9 us)
Sparse Core Ops, SparseCore 0:
  9.1 68.1 all-gather.1
where the time goes:
time: 204 us; the launch traced here: 203 us
  waiting for transfers between devices  112 us (55%)
  Pallas kernels  36.3 us (18%)
  starting transfers between devices  34.1 us (17%)
  between operations  13.8 us (7%)
  local copies, waits for them, and re-layouts  4.96 us (2%)
  other arithmetic  2.52 us (1%)
    ppermute x22, waiting for transfers between devices, move(): return lax.ppermute(array, axis, [(i, (i + by) % n) for i in range(n)])  78.7 us
    all_to_all x1, waiting for transfers between devices, local(): lax.all_to_all(direct.reshape(PAIR, SLOT, WIDTH), ('z', 'y'), split_axis=...  29.4 us
    pallas_call x3, Pallas kernels, product(): pl.pallas_call(kernel, grid_spec=pltpu.PrefetchScalarGridSpec(num_scalar_...  26.4 us
    ppermute x22, starting transfers between devices, move(): return lax.ppermute(array, axis, [(i, (i + by) % n) for i in range(n)])  24 us
    all_to_all x1, starting transfers between devices, local(): lax.all_to_all(direct.reshape(PAIR, SLOT, WIDTH), ('z', 'y'), split_axis=...  10.1 us
    pallas_call x1, Pallas kernels, turn(): pl.pallas_call(turn_kernel, in_specs=[vmem] * 3, out_specs=[vmem] * NX, o...  4.42 us
    pallas_call x1, Pallas kernels, finish(): pl.pallas_call(finish_kernel, in_specs=[vmem] * (4 + NX), out_specs=vmem,...  4.15 us
  transfers between devices with their start and end apart: 24, of which 14 were waited for; matrix products, arithmetic and copies ran while one was open for 3% of the time, Pallas kernels for 13%

commit v1 on v0

--- a/solution.py
+++ b/solution.py
@@ -19,6 +19,7 @@
 PLANE = NZ * SLOT
 PIECE = A_BLOCK * A_BLOCK
 HALF = ROWS // 2
+CHUNKS = ((0, 8), (8, 4))
 F32 = jnp.float32
 BF16 = jnp.bfloat16
 ROOM = pltpu.CompilerParams(vmem_limit_bytes=48 * 2**20)
@@ -80,64 +81,121 @@
 
 
 def total_kernel(own_ref, *refs):
-    got, out_ref = refs[:4], refs[4]
+    got, outs = refs[:4], refs[4:]
     for h in range(2):
         rows = slice(h * HALF, (h + 1) * HALF)
-        out_ref[rows, :] = (own_ref[rows, :] + got[h][...].astype(F32) + got[2 + h][...].astype(F32)).astype(BF16)
+        value = (own_ref[rows, :] + got[h][...].astype(F32) + got[2 + h][...].astype(F32)).astype(BF16)
+        for (first, count), out in zip(CHUNKS, outs):
+            out[rows, :] = value[:, first * V:(first + count) * V]
 
 
 def total(own, *got):
     vmem = pl.BlockSpec(memory_space=pltpu.VMEM)
     return pl.pallas_call(
         total_kernel,
+        in_specs=[vmem] * 5,
+        out_specs=[vmem] * len(CHUNKS),
+        out_shape=[jax.ShapeDtypeStruct((ROWS, count * V), BF16) for _, count in CHUNKS],
+        compiler_params=ROOM,
+    )(own, *got)
+
+
+def turn_kernel(send_ref, *refs):
+    outs, rows = refs[-NX:], refs[0][...]
+    if len(refs) == NX + 2:
+        rows = jnp.dot(refs[1][...], rows, preferred_element_type=F32).astype(BF16)
+    turned = lax.dot_general(send_ref[...], rows, (((1,), (1,)), ((), ())), preferred_element_type=F32).astype(BF16)
+    size = turned.shape[0] // VIRT
+    for d, out in enumerate(outs):
+        for core in range(2):
+            out[core] = turned[(2 * d + core) * size:(2 * d + core + 1) * size, :]
+
+
+def turn(send, rows, *pick):
+    vmem = pl.BlockSpec(memory_space=pltpu.VMEM)
+    return pl.pallas_call(
+        turn_kernel,
+        in_specs=[vmem] * (2 + len(pick)),
+        out_specs=[vmem] * NX,
+        out_shape=[jax.ShapeDtypeStruct((2, send.shape[0] // VIRT, ROWS), BF16)] * NX,
+        compiler_params=ROOM,
+    )(send, rows, *pick)
+
+
+def swap(sent):
+    arrived = [sent[0]] + [move(sent[d], "x", d) for d in range(1, NX)]
+    return arrived + [move(jnp.concatenate([block[1:] for block in arrived], axis=0), "c", 1)]
+
+
+def stacked(blocks, u_ref):
+    size = u_ref.shape[0] // VIRT
+    for k in range(NX):
+        u_ref[2 * k * size:(2 * k + 1) * size, :] = blocks[k][0]
+        u_ref[(2 * k + 1) * size:(2 * k + 2) * size, :] = blocks[NX][k]
+
+
+def back_kernel(*refs):
+    stacked(refs[:NX + 1], refs[-1])
+    refs[NX + 1][...] = refs[-1][...].T
+
+
+def back(blocks):
+    vmem = pl.BlockSpec(memory_space=pltpu.VMEM)
+    width = VIRT * blocks[0].shape[1]
+    return pl.pallas_call(
+        back_kernel,
+        in_specs=[vmem] * (1 + NX),
+        out_specs=vmem,
+        out_shape=jax.ShapeDtypeStruct((ROWS, width), BF16),
+        scratch_shapes=[pltpu.VMEM((width, ROWS), BF16)],
+        compiler_params=ROOM,
+    )(*blocks)
+
+
+def begin_kernel(land_ref, *refs):
+    blocks, direct, o_ref, u_ref = refs[:NX + 1], refs[NX + 1:-2], refs[-2], refs[-1]
+    stacked(blocks, u_ref)
+    o_ref[...] = lax.dot_general(u_ref[...], land_ref[...], (((0,), (0,)), ((), ())), preferred_element_type=F32)
+    for (first, count), part in zip(CHUNKS, direct):
+        at = slice(first * V, (first + count) * V)
+        o_ref[:, at] = o_ref[:, at] + part[...].astype(F32)
+
+
+def begin(land, blocks, direct):
+    vmem = pl.BlockSpec(memory_space=pltpu.VMEM)
+    return pl.pallas_call(
+        begin_kernel,
+        in_specs=[vmem] * (2 + NX + len(direct)),
+        out_specs=vmem,
+        out_shape=jax.ShapeDtypeStruct((ROWS, WIDTH), F32),
+        scratch_shapes=[pltpu.VMEM((land.shape[0], ROWS), BF16)],
+        compiler_params=ROOM,
+    )(land, *blocks, *direct)
+
+
+def finish_kernel(active_ref, begun_ref, pick_ref, land_ref, received_ref, o_ref):
+    picked = jnp.dot(pick_ref[...], received_ref[...], preferred_element_type=F32).astype(BF16)
+    value = begun_ref[...] + jnp.dot(picked, land_ref[...], preferred_element_type=F32)
+    column = lax.broadcasted_iota(jnp.int32, (ROWS, WIDTH), 1)
+    live = jnp.where(lax.rem(column, V) < TW, active_ref[:, :1], active_ref[:, 1:]) > 0
+    o_ref[...] = jnp.where(live, value, 0).astype(BF16)
+
+
+def finish(active, begun, pick, land, received):
+    vmem = pl.BlockSpec(memory_space=pltpu.VMEM)
+    return pl.pallas_call(
+        finish_kernel,
         in_specs=[vmem] * 5,
         out_specs=vmem,
         out_shape=jax.ShapeDtypeStruct((ROWS, WIDTH), BF16),
         compiler_params=ROOM,
-    )(own, *got)
-
-
-def turn_kernel(pick_ref, send_ref, received_ref, *outs):
-    picked = jnp.dot(pick_ref[...], received_ref[...], preferred_element_type=F32).astype(BF16)
-    turned = lax.dot_general(send_ref[...], picked, (((1,), (1,)), ((), ())), preferred_element_type=F32).astype(BF16)
-    for d, out in enumerate(outs):
-        for core in range(2):
-            out[core] = turned[(2 * d + core) * PIECE:(2 * d + core + 1) * PIECE, :]
-
-
-def turn(pick, send, received):
-    vmem = pl.BlockSpec(memory_space=pltpu.VMEM)
-    return pl.pallas_call(
-        turn_kernel,
-        in_specs=[vmem] * 3,
-        out_specs=[vmem] * NX,
-        out_shape=[jax.ShapeDtypeStruct((2, PIECE, ROWS), BF16)] * NX,
-        compiler_params=ROOM,
-    )(pick, send, received)
-
-
-def finish_kernel(active_ref, land_ref, direct_ref, *refs):
-    blocks, across, o_ref, u_ref = refs[:NX], *refs[NX:]
-    for k, block in enumerate(blocks):
-        u_ref[2 * k * PIECE:(2 * k + 1) * PIECE, :] = block[0]
-        u_ref[(2 * k + 1) * PIECE:(2 * k + 2) * PIECE, :] = across[k]
-    mirrored = lax.dot_general(u_ref[...], land_ref[...], (((0,), (0,)), ((), ())), preferred_element_type=F32)
-    value = direct_ref[...].astype(F32) + mirrored
-    column = lax.broadcasted_iota(jnp.int32, (ROWS, WIDTH), 1)
-    live = jnp.where(lax.rem(column, V) < TW, active_ref[:, :1], active_ref[:, 1:]) > 0
-    o_ref[...] = jnp.where(live, value, 0).astype(BF16)
-
-
-def finish(active, land, direct, blocks, across):
-    vmem = pl.BlockSpec(memory_space=pltpu.VMEM)
-    return pl.pallas_call(
-        finish_kernel,
-        in_specs=[vmem] * (4 + NX),
-        out_specs=vmem,
-        out_shape=jax.ShapeDtypeStruct((ROWS, WIDTH), BF16),
-        scratch_shapes=[pltpu.VMEM((WIDTH, ROWS), BF16)],
-        compiler_params=ROOM,
-    )(active, land, direct, *blocks, across)
+    )(active, begun, pick, land, received)
+
+
+def over_pair(rows):
+    width = rows.shape[1]
+    moved = lax.all_to_all(rows.reshape(PAIR, SLOT, width), ("z", "y"), split_axis=0, concat_axis=0, tiled=True)
+    return moved.reshape(ROWS, width)
 
 
 def local(amplitudes, block_mask, integrals, mirror):
@@ -177,17 +235,20 @@
     position = source * SLOT + mirror % ROWS - pair * SLOT
     row = jnp.arange(ROWS, dtype=jnp.int32)
     pick = (position[:, None] == row[None, :]).astype(BF16)
-    core, step, second, first = column // PIECE % 2, column // (2 * PIECE), column % PIECE // A_BLOCK, column % A_BLOCK
-    target = (x + step) % NX * 2 + (c + core) % 2
-    send = ((first * V + target * A_BLOCK + second)[:, None] == column[None, :]).astype(BF16)
-    origin = (x + NX - step) % NX * 2 + (c + core) % 2
-    land = ((second * V + origin * A_BLOCK + first)[:, None] == column[None, :]).astype(BF16)
-
-    received = lax.all_to_all(direct.reshape(PAIR, SLOT, WIDTH), ("z", "y"), split_axis=0, concat_axis=0, tiled=True)
-    sent = turn(pick, send, received.reshape(ROWS, WIDTH))
-    arrived = [sent[0]] + [move(sent[d], "x", d) for d in range(1, NX)]
-    across = move(jnp.concatenate([block[1:] for block in arrived], axis=0), "c", 1)
-    return finish(active, land, direct, arrived, across)
+    sends, lands = [], []
+    for first, count in CHUNKS:
+        slot = jnp.arange(count * V, dtype=jnp.int32)
+        size = A_BLOCK * count
+        step, core, second, inner = slot // (2 * size), slot // size % 2, slot % size // count, slot % count
+        virt = (x + step) % NX * 2 + (c + core) % 2
+        sends.append(((inner * V + virt * A_BLOCK + second)[:, None] == slot[None, :]).astype(BF16))
+        virt = (x + NX - step) % NX * 2 + (c + core) % 2
+        lands.append(((second * V + virt * A_BLOCK + first + inner)[:, None] == column[None, :]).astype(BF16))
+
+    received = over_pair(direct[1])
+    crossed = back(swap(turn(sends[0], direct[0])))
+    begun = begin(lands[1], swap(turn(sends[1], received, pick)), direct)
+    return finish(active, begun, pick, lands[0], over_pair(crossed))
 
 
 def solution(mesh):

time: 204 us -> 197 us (0.966)
  waiting for transfers between devices: 112 us -> 91.1 us
  starting transfers between devices: 34.1 us -> 44.8 us
  local copies, waits for them, and re-layouts: 4.96 us -> 7.36 us
    all_to_all x1 -> x2, waiting for transfers between devices: 29.4 us -> 15.4 us  [over_pair(): lax.all_to_all(rows.reshape(PAIR, SLOT, width), ('z', 'y'), split_axis=0,...]
    all_to_all x1 -> x2, starting transfers between devices: 10.1 us -> 16.2 us  [over_pair(): lax.all_to_all(rows.reshape(PAIR, SLOT, width), ('z', 'y'), split_axis=0,...]
    ppermute x22 -> x26, waiting for transfers between devices: 78.7 us -> 72.8 us  [move(): return lax.ppermute(array, axis, [(i, (i + by) % n) for i in range(n)])]
    ppermute x22 -> x26, starting transfers between devices: 24 us -> 28.6 us  [move(): return lax.ppermute(array, axis, [(i, (i + by) % n) for i in range(n)])]
    unnamed x21 -> x27, local copies, waits for them, and re-layouts: 1.85 us -> 4.26 us
    pallas_call x3 -> x6, Pallas kernels: 9.95 us -> 9.42 us  [the longest x1 3.8 us: finish(): pl.pallas_call(finish_kernel, in_specs=[vmem] * 5, out_specs=vmem, out_sh...]
  transfers between devices with their start and end apart: 24 -> 29, of which waited for: 14 -> 18; matrix products, arithmetic and copies ran while one was open for 3% -> 4% of each run, Pallas kernels for 13% -> 15%
where the time goes in v1:
time: 197 us
  waiting for transfers between devices  91.1 us (46%)
  starting transfers between devices  44.8 us (23%)
  Pallas kernels  35.8 us (18%)
  between operations  13.9 us (7%)
  local copies, waits for them, and re-layouts  7.36 us (4%)
  other arithmetic  3.74 us (2%)
    ppermute x26, waiting for transfers between devices, move(): return lax.ppermute(array, axis, [(i, (i + by) % n) for i in range(n)])  72.8 us
    ppermute x26, starting transfers between devices, move(): return lax.ppermute(array, axis, [(i, (i + by) % n) for i in range(n)])  28.6 us
    pallas_call x3, Pallas kernels, product(): pl.pallas_call(kernel, grid_spec=pltpu.PrefetchScalarGridSpec(num_scalar_...  26.4 us
    all_to_all x2, starting transfers between devices, over_pair(): lax.all_to_all(rows.reshape(PAIR, SLOT, width), ('z', 'y'), split_axis=0,...  16.2 us
    all_to_all x2, waiting for transfers between devices, over_pair(): lax.all_to_all(rows.reshape(PAIR, SLOT, width), ('z', 'y'), split_axis=0,...  15.4 us
    unnamed x27, local copies, waits for them, and re-layouts  4.26 us
  transfers between devices with their start and end apart: 29, of which 18 were waited for; matrix products, arithmetic and copies ran while one was open for 4% of the time, Pallas kernels for 15%

profile of v1, /device:TPU:8, one launch (start us, length us, event | category | flops | bytes accessed | tf_op | source)
XLA Modules:
  0.0 196.7 jit_solution(5668064367920472183)
XLA Ops:
  9.4 2.4 %collective-permute-start = (bf16[1,288,512]{2,1,0:T(8,128)(2,1)S(1)}, bf16[1,288,512]{2,1,0:T(8,128)(2,1)S(1)}, u32[]{:S(2)}, u32[]{:S(2)}) collective-permute-start(bf16[1,288,512]{2,1,0:T(8,128)(2,1)S(1)} %get-tuple-element.42), channel_id=1, source_target_pairs={{0,16},{8,24},{16,0},{24,8},{1,17},{9,25},{17,1},{25,9},{2,18},{10... | collective-permute-start | bytes 884744 | tf_op jit(solution)/shard_map/ppermute | solution.py:30
  13.8 7.1 %collective-permute-done = bf16[1,288,512]{2,1,0:T(8,128)(2,1)S(1)} collective-permute-done((bf16[1,288,512]{2,1,0:T(8,128)(2,1)S(1)}, bf16[1,288,512]{2,1,0:T(8,128)(2,1)S(1)}, u32[]{:S(2)}, u32[]{:S(2)}) %collective-permute-start) | collective-permute-done | bytes 294944 | tf_op jit(solution)/shard_map/ppermute | solution.py:30
  20.9 5.1 %collective-permute-done.1 = bf16[1,288,512]{2,1,0:T(8,128)(2,1)S(1)} collective-permute-done((bf16[1,288,512]{2,1,0:T(8,128)(2,1)S(1)}, bf16[1,288,512]{2,1,0:T(8,128)(2,1)S(1)}, u32[]{:S(2)}, u32[]{:S(2)}) %collective-permute-start.1) | collective-permute-done | bytes 294944 | tf_op jit(solution)/shard_map/ppermute | solution.py:30
  26.3 1.6 collective-permute-start.4
  27.9 1.7 collective-permute-start.6
  29.7 25.8 %collective-permute-done.4.refs_3_ = bf16[4,288,512]{2,1,0:T(8,128)(2,1)S(1)} collective-permute-done((bf16[4,288,512]{2,1,0:T(8,128)(2,1)S(1)}, bf16[4,288,512]{2,1,0:T(8,128)(2,1)S(1)}, u32[]{:S(2)}, u32[]{:S(2)}) %collective-permute-start.4) | collective-permute-done | bytes 1179680 | tf_op jit(solution)/shard_map/ppermute | solution.py:30
  57.1 1.9 slice.51
  59.0 2.3 %collective-permute-start.10 = (bf16[2,288,512]{2,1,0:T(8,128)(2,1)}, bf16[2,288,512]{2,1,0:T(8,128)(2,1)}, u32[]{:S(2)}, u32[]{:S(2)}) collective-permute-start(bf16[2,288,512]{2,1,0:T(8,128)(2,1)} %slice.51), channel_id=1, source_target_pairs={{0,6},{2,0},{4,2},{6,4},{1,7},{3,1},{5,3},{7,5},{8,14},{10,8},{12,... | collective-permute-start | bytes 1769480 | tf_op jit(solution)/shard_map/ppermute | solution.py:30
  61.3 11.5 %collective-permute-done.8.refs_7_ = bf16[2,288,512]{2,1,0:T(8,128)(2,1)} collective-permute-done((bf16[2,288,512]{2,1,0:T(8,128)(2,1)S(1)}, bf16[2,288,512]{2,1,0:T(8,128)(2,1)}, u32[]{:S(2)}, u32[]{:S(2)}) %collective-permute-start.8) | collective-permute-done | bytes 589856 | tf_op jit(solution)/shard_map/ppermute | solution.py:30
  72.9 1.9 collective-permute-done.10.refs_7_
  75.1 2.2 %all-gather.2.cloned.1.call-done.refs_9_ = bf16[2304,1152]{1,0:T(8,128)(2,1)} async-done(((bf16[288,1152]{1,0:T(8,128)(2,1)}), bf16[2304,1152]{1,0:T(8,128)(2,1)}) %all-gather.2.cloned.1.call-update) | async-done | bytes 5308432 | tf_op jit(solution)/shard_map/all_gather | solution.py:209
  77.3 6.9 %shard_map.46 = (bf16[256,1152]{1,0:T(8,128)(2,1)S(1)}, bf16[256,1152]{1,0:T(8,128)(2,1)S(1)}) custom-call(s32[8]{0:T(128)S(1)} %stack.35.refs_0_, bf16[4,288,512]{2,1,0:T(8,128)(2,1)S(1)} %pad_maximum_fusion.refs_1_, bf16[4,288,512]{2,1,0:T(8,128)(2,1)S(1)} %collective-permute-done.3.refs_2_, bf16[4,288,512]{2,1,0:T(8,128)(2,1)S(1)} %collective-permute-done.4.refs_3_, ...), custom_call_target="tpu_custom_call" | custom-call | tf_op jit(solution)/shard_map/pallas_call | solution.py:55
  84.9 1.5 collective-permute-start.12
  86.4 11.1 %shard_map.47 = (bf16[256,1152]{1,0:T(8,128)(2,1)S(1)}, bf16[256,1152]{1,0:T(8,128)(2,1)S(1)}, bf16[256,1152]{1,0:T(8,128)(2,1)S(1)}, bf16[256,1152]{1,0:T(8,128)(2,1)S(1)}) custom-call(s32[8]{0:T(128)S(1)} %stack.35.refs_0_, bf16[4,288,512]{2,1,0:T(8,128)(2,1)S(1)} %pad_maximum_fusion.refs_1_, bf16[4,288,512]{2,1,0:T(8,128)(2,1)} %copy-done.3, ...), custom_call_target="tpu_custom_call" | custom-call | tf_op jit(solution)/shard_map/pallas_call | solution.py:55
  97.5 1.6 collective-permute-start.15
  99.8 2.6 %collective-permute-start.17 = (bf16[256,1152]{1,0:T(8,128)(2,1)S(1)}, bf16[256,1152]{1,0:T(8,128)(2,1)S(1)}, u32[]{:S(2)}, u32[]{:S(2)}) collective-permute-start(bf16[256,1152]{1,0:T(8,128)(2,1)S(1)} %add_convert_fusion.refs_11_), channel_id=1, source_target_pairs={{0,24},{8,0},{16,8},{24,16},{1,25},{9,1},{17,9},{25,17},{2,26},{10... | collective-permute-start | bytes 1769480 | tf_op jit(solution)/shard_map/ppermute | solution.py:30
  104.0 8.3 %shard_map.48.own_ref = f32[512,1152]{1,0:T(8,128)} custom-call(s32[8]{0:T(128)S(1)} %stack.35.refs_0_, bf16[4,288,512]{2,1,0:T(8,128)(2,1)S(1)} %pad_maximum_fusion.refs_1_, bf16[4,288,512]{2,1,0:T(8,128)(2,1)S(1)} %copy-done.4, bf16[4,288,512]{2,1,0:T(8,128)(2,1)S(1)} %copy-done.2, bf16[4,288,512]{2,1,0:T(8,128)(2,1)} %collective-permute-done.5.refs_4_, ...), custom_call_target="tpu_custom_call" | custom-call | tf_op jit(solution)/shard_map/pallas_call | solution.py:55
  112.4 2.1 %collective-permute-done.15.refs_1_ = bf16[256,1152]{1,0:T(8,128)(2,1)S(1)} collective-permute-done((bf16[256,1152]{1,0:T(8,128)(2,1)S(1)}, bf16[256,1152]{1,0:T(8,128)(2,1)S(1)}, u32[]{:S(2)}, u32[]{:S(2)}) %collective-permute-start.15) | collective-permute-done | bytes 589856 | tf_op jit(solution)/shard_map/ppermute | solution.py:30
  115.7 10.9 %collective-permute-done.17.refs_3_ = bf16[256,1152]{1,0:T(8,128)(2,1)S(1)} collective-permute-done((bf16[256,1152]{1,0:T(8,128)(2,1)S(1)}, bf16[256,1152]{1,0:T(8,128)(2,1)S(1)}, u32[]{:S(2)}, u32[]{:S(2)}) %collective-permute-start.17) | collective-permute-done | bytes 589856 | tf_op jit(solution)/shard_map/ppermute | solution.py:30
  126.6 1.7 copy-done.5
  130.2 1.5 collective-permute-start.22
  131.7 2.7 %collective-permute-start.23 = (bf16[2,96,512]{2,1,0:T(8,128)(2,1)S(1)}, bf16[2,96,512]{2,1,0:T(8,128)(2,1)S(1)}, u32[]{:S(2)}, u32[]{:S(2)}) collective-permute-start(bf16[2,96,512]{2,1,0:T(8,128)(2,1)S(1)} %get-tuple-element.35), channel_id=1, source_target_pairs={{0,4},{2,6},{4,0},{6,2},{1,5},{3,7},{5,1},{7,3},{8,12},{10,14},{12... | collective-permute-start | bytes 589832 | tf_op jit(solution)/shard_map/ppermute | solution.py:30
  135.8 10.4 %all-to-all-start = ((bf16[32,16,384]{2,1,0:T(8,128)(2,1)}), bf16[32,16,384]{2,1,0:T(8,128)(2,1)S(1)}, u32[]{:S(2)}, u32[]{:S(2)}) async-start(bf16[32,16,384]{2,1,0:T(8,128)(2,1)} %bitcast.10), calls=%async_computation | async-start | bytes 786432 | tf_op jit(solution)/shard_map/all_to_all | solution.py:197
  146.8 1.5 collective-permute-done.25.refs_4_
  149.4 9.3 %all-to-all-done = bf16[32,16,384]{2,1,0:T(8,128)(2,1)S(1)} async-done(((bf16[32,16,384]{2,1,0:T(8,128)(2,1)}), bf16[32,16,384]{2,1,0:T(8,128)(2,1)S(1)}, u32[]{:S(2)}, u32[]{:S(2)}) %all-to-all-start) | async-done | bytes 393248 | tf_op jit(solution)/shard_map/all_to_all | solution.py:197
  158.7 5.7 %all-to-all-start.1 = ((bf16[32,16,768]{2,1,0:T(8,128)(2,1)}), bf16[32,16,768]{2,1,0:T(8,128)(2,1)}, u32[]{:S(2)}, u32[]{:S(2)}) async-start(bf16[32,16,768]{2,1,0:T(8,128)(2,1)} %bitcast.12), calls=%async_computation.1 | async-start | bytes 1572864 | tf_op jit(solution)/shard_map/all_to_all | solution.py:197
  164.7 1.6 fusion.land_ref
  168.8 2.1 %collective-permute-start.20 = (bf16[2,48,512]{2,1,0:T(8,128)(2,1)S(1)}, bf16[2,48,512]{2,1,0:T(8,128)(2,1)S(1)}, u32[]{:S(2)}, u32[]{:S(2)}) collective-permute-start(bf16[2,48,512]{2,1,0:T(8,128)(2,1)S(1)} %get-tuple-element.31), channel_id=1, source_target_pairs={{0,6},{2,0},{4,2},{6,4},{1,7},{3,1},{5,3},{7,5},{8,14},{10,8},{12,... | collective-permute-start | bytes 294920 | tf_op jit(solution)/shard_map/ppermute | solution.py:30
  170.9 2.0 %collective-permute-done.18.refs_1_ = bf16[2,48,512]{2,1,0:T(8,128)(2,1)S(1)} collective-permute-done((bf16[2,48,512]{2,1,0:T(8,128)(2,1)S(1)}, bf16[2,48,512]{2,1,0:T(8,128)(2,1)S(1)}, u32[]{:S(2)}, u32[]{:S(2)}) %collective-permute-start.18) | collective-permute-done | bytes 98336 | tf_op jit(solution)/shard_map/ppermute | solution.py:30
  176.7 1.8 shard_map.51.begun_ref
  178.5 6.1 %all-to-all-done.1 = bf16[32,16,768]{2,1,0:T(8,128)(2,1)} async-done(((bf16[32,16,768]{2,1,0:T(8,128)(2,1)}), bf16[32,16,768]{2,1,0:T(8,128)(2,1)}, u32[]{:S(2)}, u32[]{:S(2)}) %all-to-all-start.1) | async-done | bytes 786464 | tf_op jit(solution)/shard_map/all_to_all | solution.py:197
  186.1 3.8 %shard_map.54 = bf16[512,1152]{1,0:T(8,128)(2,1)} custom-call(s32[512,2]{1,0:T(8,128)S(1)} %copy-done.8, f32[512,1152]{1,0:T(8,128)S(1)} %shard_map.51.begun_ref, bf16[512,512]{1,0:T(8,128)(2,1)S(1)} %fusion.5.refs_1_.pick_ref, bf16[768,1152]{1,0:T(8,128)(2,1)S(1)} %copy-done.6, bf16[512,768]{1,0:T(8,128)(2,1)} %bitcast.13.received_ref), custom_call_target="tpu_custom_call" | custom-call | tf_op jit(solution)/shard_map/pallas_call | solution.py:186
  (95 shorter events, 24.0 us)
Async XLA Ops:
  6.5 70.8 %all-gather.2.cloned.1.call-start = ((), (), s32[]{:S(2)}) async-start(), calls=%async_computation.2 | async-start | bytes 5971968 | tf_op jit(solution)/shard_map/all_gather | solution.py:209
  9.4 11.5 %collective-permute-start = (bf16[1,288,512]{2,1,0:T(8,128)(2,1)S(1)}, bf16[1,288,512]{2,1,0:T(8,128)(2,1)S(1)}, u32[]{:S(2)}, u32[]{:S(2)}) collective-permute-start(bf16[1,288,512]{2,1,0:T(8,128)(2,1)S(1)} %get-tuple-element.42), channel_id=1, source_target_pairs={{0,16},{8,24},{16,0},{24,8},{1,17},{9,25},{17,1},{25,9},{2,18},{10... | collective-permute-start | bytes 884744 | tf_op jit(solution)/shard_map/ppermute | solution.py:30
  11.8 14.3 %collective-permute-start.1 = (bf16[1,288,512]{2,1,0:T(8,128)(2,1)S(1)}, bf16[1,288,512]{2,1,0:T(8,128)(2,1)S(1)}, u32[]{:S(2)}, u32[]{:S(2)}) collective-permute-start(bf16[1,288,512]{2,1,0:T(8,128)(2,1)S(1)} %get-tuple-element.41), channel_id=1, source_target_pairs={{0,24},{8,0},{16,8},{24,16},{1,25},{9,1},{17,9},{25,17},{2,26},{10... | collective-permute-start | bytes 884744 | tf_op jit(solution)/shard_map/ppermute | solution.py:30
  13.1 13.1 %collective-permute-start.2 = (bf16[1,288,512]{2,1,0:T(8,128)(2,1)S(1)}, bf16[1,288,512]{2,1,0:T(8,128)(2,1)S(1)}, u32[]{:S(2)}, u32[]{:S(2)}) collective-permute-start(bf16[1,288,512]{2,1,0:T(8,128)(2,1)S(1)} %get-tuple-element.40), channel_id=1, source_target_pairs={{0,8},{8,16},{16,24},{24,0},{1,9},{9,17},{17,25},{25,1},{2,10},{10... | collective-permute-start | bytes 884744 | tf_op jit(solution)/shard_map/ppermute | solution.py:30
  26.3 29.1 %collective-permute-start.4 = (bf16[4,288,512]{2,1,0:T(8,128)(2,1)S(1)}, bf16[4,288,512]{2,1,0:T(8,128)(2,1)S(1)}, u32[]{:S(2)}, u32[]{:S(2)}) collective-permute-start(bf16[4,288,512]{2,1,0:T(8,128)(2,1)S(1)} %pad_maximum_fusion.refs_1_), channel_id=1, source_target_pairs={{0,2},{2,4},{4,6},{6,0},{1,3},{3,5},{5,7},{7,1},{8,10},{10,12},{12... | collective-permute-start | bytes 3538952 | tf_op jit(solution)/shard_map/ppermute | solution.py:30
  27.9 27.7 %collective-permute-start.6 = (bf16[4,288,512]{2,1,0:T(8,128)(2,1)S(1)}, bf16[4,288,512]{2,1,0:T(8,128)(2,1)}, u32[]{:S(2)}, u32[]{:S(2)}) collective-permute-start(bf16[4,288,512]{2,1,0:T(8,128)(2,1)S(1)} %pad_maximum_fusion.refs_1_), channel_id=1, source_target_pairs={{0,6},{2,0},{4,2},{6,4},{1,7},{3,1},{5,3},{7,5},{8,14},{10,8},{12,... | collective-permute-start | bytes 3538952 | tf_op jit(solution)/shard_map/ppermute | solution.py:30
  29.7 45.1 %collective-permute-start.3 = (bf16[4,288,512]{2,1,0:T(8,128)(2,1)S(1)}, bf16[4,288,512]{2,1,0:T(8,128)(2,1)S(1)}, u32[]{:S(2)}, u32[]{:S(2)}) collective-permute-start(bf16[4,288,512]{2,1,0:T(8,128)(2,1)S(1)} %pad_maximum_fusion.refs_1_), channel_id=1, source_target_pairs={{0,1},{1,0},{2,3},{3,2},{4,5},{5,4},{6,7},{7,6},{8,9},{9,8},{10,11... | collective-permute-start | bytes 3538952 | tf_op jit(solution)/shard_map/ppermute | solution.py:30
  55.5 21.9 %copy-start.1 = (bf16[4,288,512]{2,1,0:T(8,128)(2,1)}, bf16[4,288,512]{2,1,0:T(8,128)(2,1)S(1)}, u32[]{:S(2)}) copy-start(bf16[4,288,512]{2,1,0:T(8,128)(2,1)S(1)} %collective-permute-done.4.refs_3_) | copy-start | bytes 3538948
  55.5 19.3 %collective-permute-start.5 = (bf16[4,288,512]{2,1,0:T(8,128)(2,1)S(1)}, bf16[4,288,512]{2,1,0:T(8,128)(2,1)}, u32[]{:S(2)}, u32[]{:S(2)}) collective-permute-start(bf16[4,288,512]{2,1,0:T(8,128)(2,1)S(1)} %collective-permute-done.4.refs_3_), channel_id=1, source_target_pairs={{0,1},{1,0},{2,3},{3,2},{4,5},{5,4},{6,7},{7,6},{8,9},{9,8},{10,11... | collective-permute-start | bytes 3538952 | tf_op jit(solution)/shard_map/ppermute | solution.py:30
  55.6 19.2 %collective-permute-start.7 = (bf16[4,288,512]{2,1,0:T(8,128)(2,1)}, bf16[4,288,512]{2,1,0:T(8,128)(2,1)}, u32[]{:S(2)}, u32[]{:S(2)}) collective-permute-start(bf16[4,288,512]{2,1,0:T(8,128)(2,1)} %collective-permute-done.6.refs_5_), channel_id=1, source_target_pairs={{0,1},{1,0},{2,3},{3,2},{4,5},{5,4},{6,7},{7,6},{8,9},{9,8},{10,11... | collective-permute-start | bytes 3538952 | tf_op jit(solution)/shard_map/ppermute | solution.py:30
  56.1 16.7 %collective-permute-start.8 = (bf16[2,288,512]{2,1,0:T(8,128)(2,1)S(1)}, bf16[2,288,512]{2,1,0:T(8,128)(2,1)}, u32[]{:S(2)}, u32[]{:S(2)}) collective-permute-start(bf16[2,288,512]{2,1,0:T(8,128)(2,1)S(1)} %slice.50), channel_id=1, source_target_pairs={{0,2},{2,4},{4,6},{6,0},{1,3},{3,5},{5,7},{7,1},{8,10},{10,12},{12... | collective-permute-start | bytes 1769480 | tf_op jit(solution)/shard_map/ppermute | solution.py:30
  59.0 15.8 %collective-permute-start.10 = (bf16[2,288,512]{2,1,0:T(8,128)(2,1)}, bf16[2,288,512]{2,1,0:T(8,128)(2,1)}, u32[]{:S(2)}, u32[]{:S(2)}) collective-permute-start(bf16[2,288,512]{2,1,0:T(8,128)(2,1)} %slice.51), channel_id=1, source_target_pairs={{0,6},{2,0},{4,2},{6,4},{1,7},{3,1},{5,3},{7,5},{8,14},{10,8},{12,... | collective-permute-start | bytes 1769480 | tf_op jit(solution)/shard_map/ppermute | solution.py:30
  72.8 2.3 %collective-permute-start.9 = (bf16[2,288,512]{2,1,0:T(8,128)(2,1)}, bf16[2,288,512]{2,1,0:T(8,128)(2,1)}, u32[]{:S(2)}, u32[]{:S(2)}) collective-permute-start(bf16[2,288,512]{2,1,0:T(8,128)(2,1)} %collective-permute-done.8.refs_7_), channel_id=1, source_target_pairs={{0,1},{1,0},{2,3},{3,2},{4,5},{5,4},{6,7},{7,6},{8,9},{9,8},{10,11... | collective-permute-start | bytes 1769480 | tf_op jit(solution)/shard_map/ppermute | solution.py:30
  74.8 11.6 %collective-permute-start.11 = (bf16[2,288,512]{2,1,0:T(8,128)(2,1)}, bf16[2,288,512]{2,1,0:T(8,128)(2,1)}, u32[]{:S(2)}, u32[]{:S(2)}) collective-permute-start(bf16[2,288,512]{2,1,0:T(8,128)(2,1)} %collective-permute-done.10.refs_7_), channel_id=1, source_target_pairs={{0,1},{1,0},{2,3},{3,2},{4,5},{5,4},{6,7},{7,6},{8,9},{9,8},{10,11... | collective-permute-start | bytes 1769480 | tf_op jit(solution)/shard_map/ppermute | solution.py:30
  84.3 15.3 %collective-permute-start.13 = (bf16[256,1152]{1,0:T(8,128)(2,1)S(1)}, bf16[256,1152]{1,0:T(8,128)(2,1)S(1)}, u32[]{:S(2)}, u32[]{:S(2)}) collective-permute-start(bf16[256,1152]{1,0:T(8,128)(2,1)S(1)} %get-tuple-element.24), channel_id=1, source_target_pairs={{0,24},{8,0},{16,8},{24,16},{1,25},{9,1},{17,9},{25,17},{2,26},{10... | collective-permute-start | bytes 1769480 | tf_op jit(solution)/shard_map/ppermute | solution.py:30
  84.9 17.5 %collective-permute-start.12 = (bf16[256,1152]{1,0:T(8,128)(2,1)S(1)}, bf16[256,1152]{1,0:T(8,128)(2,1)S(1)}, u32[]{:S(2)}, u32[]{:S(2)}) collective-permute-start(bf16[256,1152]{1,0:T(8,128)(2,1)S(1)} %get-tuple-element.21.refs_10_), channel_id=1, source_target_pairs={{0,8},{8,16},{16,24},{24,0},{1,9},{9,17},{17,25},{25,1},{2,10},{10... | collective-permute-start | bytes 1769480 | tf_op jit(solution)/shard_map/ppermute | solution.py:30
  97.5 17.0 %collective-permute-start.15 = (bf16[256,1152]{1,0:T(8,128)(2,1)S(1)}, bf16[256,1152]{1,0:T(8,128)(2,1)S(1)}, u32[]{:S(2)}, u32[]{:S(2)}) collective-permute-start(bf16[256,1152]{1,0:T(8,128)(2,1)S(1)} %get-tuple-element.25), channel_id=1, source_target_pairs={{0,8},{8,16},{16,24},{24,0},{1,9},{9,17},{17,25},{25,1},{2,10},{10... | collective-permute-start | bytes 1769480 | tf_op jit(solution)/shard_map/ppermute | solution.py:30
  99.1 16.6 %collective-permute-start.16 = (bf16[256,1152]{1,0:T(8,128)(2,1)S(1)}, bf16[256,1152]{1,0:T(8,128)(2,1)S(1)}, u32[]{:S(2)}, u32[]{:S(2)}) collective-permute-start(bf16[256,1152]{1,0:T(8,128)(2,1)S(1)} %get-tuple-element.26), channel_id=1, source_target_pairs={{0,24},{8,0},{16,8},{24,16},{1,25},{9,1},{17,9},{25,17},{2,26},{10... | collective-permute-start | bytes 1769480 | tf_op jit(solution)/shard_map/ppermute | solution.py:30
  99.8 26.8 %collective-permute-start.17 = (bf16[256,1152]{1,0:T(8,128)(2,1)S(1)}, bf16[256,1152]{1,0:T(8,128)(2,1)S(1)}, u32[]{:S(2)}, u32[]{:S(2)}) collective-permute-start(bf16[256,1152]{1,0:T(8,128)(2,1)S(1)} %add_convert_fusion.refs_11_), channel_id=1, source_target_pairs={{0,24},{8,0},{16,8},{24,16},{1,25},{9,1},{17,9},{25,17},{2,26},{10... | collective-permute-start | bytes 1769480 | tf_op jit(solution)/shard_map/ppermute | solution.py:30
  102.5 24.1 %collective-permute-start.14 = (bf16[256,1152]{1,0:T(8,128)(2,1)S(1)}, bf16[256,1152]{1,0:T(8,128)(2,1)S(1)}, u32[]{:S(2)}, u32[]{:S(2)}) collective-permute-start(bf16[256,1152]{1,0:T(8,128)(2,1)S(1)} %add_convert_fusion.1.refs_10_), channel_id=1, source_target_pairs={{0,8},{8,16},{16,24},{24,0},{1,9},{9,17},{17,25},{25,1},{2,10},{10... | collective-permute-start | bytes 1769480 | tf_op jit(solution)/shard_map/ppermute | solution.py:30
  130.2 16.1 %collective-permute-start.22 = (bf16[2,96,512]{2,1,0:T(8,128)(2,1)S(1)}, bf16[2,96,512]{2,1,0:T(8,128)(2,1)S(1)}, u32[]{:S(2)}, u32[]{:S(2)}) collective-permute-start(bf16[2,96,512]{2,1,0:T(8,128)(2,1)S(1)} %get-tuple-element.34), channel_id=1, source_target_pairs={{0,2},{2,4},{4,6},{6,0},{1,3},{3,5},{5,7},{7,1},{8,10},{10,12},{12... | collective-permute-start | bytes 589832 | tf_op jit(solution)/shard_map/ppermute | solution.py:30
  131.7 14.7 %collective-permute-start.23 = (bf16[2,96,512]{2,1,0:T(8,128)(2,1)S(1)}, bf16[2,96,512]{2,1,0:T(8,128)(2,1)S(1)}, u32[]{:S(2)}, u32[]{:S(2)}) collective-permute-start(bf16[2,96,512]{2,1,0:T(8,128)(2,1)S(1)} %get-tuple-element.35), channel_id=1, source_target_pairs={{0,4},{2,6},{4,0},{6,2},{1,5},{3,7},{5,1},{7,3},{8,12},{10,14},{12... | collective-permute-start | bytes 589832 | tf_op jit(solution)/shard_map/ppermute | solution.py:30
  134.4 12.0 %collective-permute-start.24 = (bf16[2,96,512]{2,1,0:T(8,128)(2,1)S(1)}, bf16[2,96,512]{2,1,0:T(8,128)(2,1)S(1)}, u32[]{:S(2)}, u32[]{:S(2)}) collective-permute-start(bf16[2,96,512]{2,1,0:T(8,128)(2,1)S(1)} %get-tuple-element.36), channel_id=1, source_target_pairs={{0,6},{2,0},{4,2},{6,4},{1,7},{3,1},{5,3},{7,5},{8,14},{10,8},{12,... | collective-permute-start | bytes 589832 | tf_op jit(solution)/shard_map/ppermute | solution.py:30
  135.8 10.7 %copy-start.12 = (s32[512]{0:T(512)S(1)}, s32[512]{0:T(512)}, u32[]{:S(2)}) copy-start(s32[512]{0:T(512)} %param.7) | copy-start | bytes 6148
  135.8 22.9 %all-to-all-start = ((bf16[32,16,384]{2,1,0:T(8,128)(2,1)}), bf16[32,16,384]{2,1,0:T(8,128)(2,1)S(1)}, u32[]{:S(2)}, u32[]{:S(2)}) async-start(bf16[32,16,384]{2,1,0:T(8,128)(2,1)} %bitcast.10), calls=%async_computation | async-start | bytes 786432 | tf_op jit(solution)/shard_map/all_to_all | solution.py:197
  146.5 1.8 collective-permute-start.25
  158.7 25.9 %all-to-all-start.1 = ((bf16[32,16,768]{2,1,0:T(8,128)(2,1)}), bf16[32,16,768]{2,1,0:T(8,128)(2,1)}, u32[]{:S(2)}, u32[]{:S(2)}) async-start(bf16[32,16,768]{2,1,0:T(8,128)(2,1)} %bitcast.12), calls=%async_computation.1 | async-start | bytes 1572864 | tf_op jit(solution)/shard_map/all_to_all | solution.py:197
  166.2 10.4 %copy-start.10 = (bf16[512,768]{1,0:T(8,128)(2,1)S(1)}, bf16[512,768]{1,0:T(8,128)(2,1)}, u32[]{:S(2)}) copy-start(bf16[512,768]{1,0:T(8,128)(2,1)} %copy-done.9) | copy-start | bytes 2359300
  167.0 5.9 %collective-permute-start.18 = (bf16[2,48,512]{2,1,0:T(8,128)(2,1)S(1)}, bf16[2,48,512]{2,1,0:T(8,128)(2,1)S(1)}, u32[]{:S(2)}, u32[]{:S(2)}) collective-permute-start(bf16[2,48,512]{2,1,0:T(8,128)(2,1)S(1)} %get-tuple-element.29), channel_id=1, source_target_pairs={{0,2},{2,4},{4,6},{6,0},{1,3},{3,5},{5,7},{7,1},{8,10},{10,12},{12... | collective-permute-start | bytes 294920 | tf_op jit(solution)/shard_map/ppermute | solution.py:30
  168.1 6.1 %collective-permute-start.19 = (bf16[2,48,512]{2,1,0:T(8,128)(2,1)S(1)}, bf16[2,48,512]{2,1,0:T(8,128)(2,1)S(1)}, u32[]{:S(2)}, u32[]{:S(2)}) collective-permute-start(bf16[2,48,512]{2,1,0:T(8,128)(2,1)S(1)} %get-tuple-element.30), channel_id=1, source_target_pairs={{0,4},{2,6},{4,0},{6,2},{1,5},{3,7},{5,1},{7,3},{8,12},{10,14},{12... | collective-permute-start | bytes 294920 | tf_op jit(solution)/shard_map/ppermute | solution.py:30
  168.8 6.0 %collective-permute-start.20 = (bf16[2,48,512]{2,1,0:T(8,128)(2,1)S(1)}, bf16[2,48,512]{2,1,0:T(8,128)(2,1)S(1)}, u32[]{:S(2)}, u32[]{:S(2)}) collective-permute-start(bf16[2,48,512]{2,1,0:T(8,128)(2,1)S(1)} %get-tuple-element.31), channel_id=1, source_target_pairs={{0,6},{2,0},{4,2},{6,4},{1,7},{3,1},{5,3},{7,5},{8,14},{10,8},{12,... | collective-permute-start | bytes 294920 | tf_op jit(solution)/shard_map/ppermute | solution.py:30
  174.9 1.8 collective-permute-start.21
  (10 other events, 28.8 us)
Sparse Core Ops, SparseCore 0:
  9.1 68.1 all-gather.1

commit v2 on v1

--- a/solution.py
+++ b/solution.py
@@ -76,28 +76,46 @@
     return [b for one in (block, left, right, far_low, far_high) for b in (one, move(one, "c", 1))]
 
 
-def joined(near, far):
-    return (near.astype(F32) + far.astype(F32)).astype(BF16)
-
-
-def total_kernel(own_ref, *refs):
-    got, outs = refs[:4], refs[4:]
-    for h in range(2):
-        rows = slice(h * HALF, (h + 1) * HALF)
-        value = (own_ref[rows, :] + got[h][...].astype(F32) + got[2 + h][...].astype(F32)).astype(BF16)
-        for (first, count), out in zip(CHUNKS, outs):
-            out[rows, :] = value[:, first * V:(first + count) * V]
-
-
-def total(own, *got):
-    vmem = pl.BlockSpec(memory_space=pltpu.VMEM)
-    return pl.pallas_call(
-        total_kernel,
-        in_specs=[vmem] * 5,
-        out_specs=[vmem] * len(CHUNKS),
-        out_shape=[jax.ShapeDtypeStruct((ROWS, count * V), BF16) for _, count in CHUNKS],
-        compiler_params=ROOM,
-    )(own, *got)
+def combine_kernel(up_ref, down_ref, from_down_ref, from_up_ref, *outs):
+    first = pl.program_id(0) == 0
+    up = (up_ref[...].astype(F32) + jnp.where(first, from_down_ref[...].astype(F32), 0)).astype(BF16)
+    down = (down_ref[...].astype(F32) + jnp.where(first, 0, from_up_ref[...].astype(F32))).astype(BF16)
+    for n, (at, count) in enumerate(CHUNKS):
+        outs[2 * n][...] = up[:, at * V:(at + count) * V]
+        outs[2 * n + 1][...] = down[:, at * V:(at + count) * V]
+
+
+def combine(up, down, from_down, from_up):
+    fixed = pl.BlockSpec((HALF, WIDTH), lambda i: (0, 0))
+    moving = pl.BlockSpec((HALF, WIDTH), lambda i: (i, 0))
+    widths = [count * V for _, count in CHUNKS for _ in range(2)]
+    return pl.pallas_call(
+        combine_kernel,
+        grid=(2,),
+        in_specs=[moving] * 2 + [fixed] * 2,
+        out_specs=[pl.BlockSpec((HALF, w), lambda i: (i, 0)) for w in widths],
+        out_shape=[jax.ShapeDtypeStruct((ROWS, w), BF16) for w in widths],
+        compiler_params=ROOM,
+    )(up, down, from_down, from_up)
+
+
+def total_kernel(at, own_ref, down_ref, up_ref, out_ref):
+    out_ref[...] = (own_ref[:, at] + down_ref[...].astype(F32) + up_ref[...].astype(F32)).astype(BF16)
+
+
+def total(at, own, got_down, got_up):
+    vmem = pl.BlockSpec(memory_space=pltpu.VMEM)
+
+    def kernel(*refs):
+        total_kernel(at, *refs)
+
+    return pl.pallas_call(
+        kernel,
+        in_specs=[vmem] * 3,
+        out_specs=vmem,
+        out_shape=jax.ShapeDtypeStruct((ROWS, at.stop - at.start), BF16),
+        compiler_params=ROOM,
+    )(own, got_down, got_up)
 
 
 def turn_kernel(send_ref, *refs):
@@ -222,14 +240,13 @@
     far_low, far_high = product(where, 1, 1, low, whole, 2, BF16)
     from_down = move(far_low, "y", 1)
     from_up = move(far_high, "y", -1)
-    up_low, up_high, down_low, down_high = product(where, 2, 2, high, whole, 2, BF16, far_low)
-    from_down_high = move(up_high, "y", 1)
-    from_up_low = move(down_low, "y", -1)
-    up_low, down_high = joined(up_low, from_down), joined(down_high, from_up)
-    from_down_low = move(up_low, "y", 1)
-    from_up_high = move(down_high, "y", -1)
-    own, = product(where, 0, 1, low, whole, 1, F32, up_low, down_high)
-    direct = total(own, from_down_low, from_down_high, from_up_low, from_up_high)
+    up, down = product(where, 2, 2, high, whole, 1, BF16, far_low)
+    up_last, down_last, up_first, down_first = combine(up, down, from_down, from_up)
+    first = move(up_first, "y", 1), move(down_first, "y", -1)
+    last = move(up_last, "y", 1), move(down_last, "y", -1)
+    own, = product(where, 0, 1, low, whole, 1, F32, up_first)
+    parts = [slice(first * V, (first + count) * V) for first, count in CHUNKS]
+    direct = [total(parts[0], own, *last), total(parts[1], own, *first)]
 
     source = mirror // ROWS
     position = source * SLOT + mirror % ROWS - pair * SLOT

time: 197 us -> 195 us (0.990); the launches traced: 197 us -> 192 us
  waiting for transfers between devices: 91.1 us -> 85.1 us
    all_to_all x2, waiting for transfers between devices: 15.4 us -> 11.9 us  [over_pair(): lax.all_to_all(rows.reshape(PAIR, SLOT, width), ('z', 'y'), split_axis=0,...]
    ppermute x26, waiting for transfers between devices: 72.8 us -> 70.3 us  [move(): return lax.ppermute(array, axis, [(i, (i + by) % n) for i in range(n)])]
    unnamed x27 -> x29, local copies, waits for them, and re-layouts: 4.26 us -> 4.37 us
  transfers between devices with their start and end apart: 29 -> 29, of which waited for: 18 -> 19; matrix products, arithmetic and copies ran while one was open for 4% -> 4% of each run, Pallas kernels for 15% -> 17%
where the time goes in v2:
time: 195 us; the launch traced here: 192 us
  waiting for transfers between devices  85.1 us (44%)
  starting transfers between devices  44.8 us (23%)
  Pallas kernels  37.2 us (19%)
  between operations  13.9 us (7%)
  local copies, waits for them, and re-layouts  7.47 us (4%)
  other arithmetic  3.47 us (2%)
    ppermute x26, waiting for transfers between devices, move(): return lax.ppermute(array, axis, [(i, (i + by) % n) for i in range(n)])  70.3 us
    ppermute x26, starting transfers between devices, move(): return lax.ppermute(array, axis, [(i, (i + by) % n) for i in range(n)])  28.7 us
    pallas_call x3, Pallas kernels, product(): pl.pallas_call(kernel, grid_spec=pltpu.PrefetchScalarGridSpec(num_scalar_...  26.4 us
    all_to_all x2, starting transfers between devices, over_pair(): lax.all_to_all(rows.reshape(PAIR, SLOT, width), ('z', 'y'), split_axis=0,...  16.1 us
    all_to_all x2, waiting for transfers between devices, over_pair(): lax.all_to_all(rows.reshape(PAIR, SLOT, width), ('z', 'y'), split_axis=0,...  11.9 us
    unnamed x29, local copies, waits for them, and re-layouts  4.37 us
  transfers between devices with their start and end apart: 29, of which 19 were waited for; matrix products, arithmetic and copies ran while one was open for 4% of the time, Pallas kernels for 17%

profile of v2, /device:TPU:8, one launch (start us, length us, event | category | flops | bytes accessed | tf_op | source)
XLA Modules:
  0.0 192.0 jit_solution(7551768472666121421)
XLA Ops:
  9.4 2.4 %collective-permute-start = (bf16[1,288,512]{2,1,0:T(8,128)(2,1)S(1)}, bf16[1,288,512]{2,1,0:T(8,128)(2,1)S(1)}, u32[]{:S(2)}, u32[]{:S(2)}) collective-permute-start(bf16[1,288,512]{2,1,0:T(8,128)(2,1)S(1)} %get-tuple-element.42), channel_id=1, source_target_pairs={{0,16},{8,24},{16,0},{24,8},{1,17},{9,25},{17,1},{25,9},{2,18},{10... | collective-permute-start | bytes 884744 | tf_op jit(solution)/shard_map/ppermute | solution.py:30
  13.8 7.1 %collective-permute-done = bf16[1,288,512]{2,1,0:T(8,128)(2,1)S(1)} collective-permute-done((bf16[1,288,512]{2,1,0:T(8,128)(2,1)S(1)}, bf16[1,288,512]{2,1,0:T(8,128)(2,1)S(1)}, u32[]{:S(2)}, u32[]{:S(2)}) %collective-permute-start) | collective-permute-done | bytes 294944 | tf_op jit(solution)/shard_map/ppermute | solution.py:30
  20.9 5.1 %collective-permute-done.1 = bf16[1,288,512]{2,1,0:T(8,128)(2,1)S(1)} collective-permute-done((bf16[1,288,512]{2,1,0:T(8,128)(2,1)S(1)}, bf16[1,288,512]{2,1,0:T(8,128)(2,1)S(1)}, u32[]{:S(2)}, u32[]{:S(2)}) %collective-permute-start.1) | collective-permute-done | bytes 294944 | tf_op jit(solution)/shard_map/ppermute | solution.py:30
  26.3 1.6 collective-permute-start.4
  27.9 1.7 collective-permute-start.6
  29.7 25.8 %collective-permute-done.4.refs_3_ = bf16[4,288,512]{2,1,0:T(8,128)(2,1)S(1)} collective-permute-done((bf16[4,288,512]{2,1,0:T(8,128)(2,1)S(1)}, bf16[4,288,512]{2,1,0:T(8,128)(2,1)S(1)}, u32[]{:S(2)}, u32[]{:S(2)}) %collective-permute-start.4) | collective-permute-done | bytes 1179680 | tf_op jit(solution)/shard_map/ppermute | solution.py:30
  57.1 1.9 slice.51
  59.0 2.3 %collective-permute-start.10 = (bf16[2,288,512]{2,1,0:T(8,128)(2,1)}, bf16[2,288,512]{2,1,0:T(8,128)(2,1)}, u32[]{:S(2)}, u32[]{:S(2)}) collective-permute-start(bf16[2,288,512]{2,1,0:T(8,128)(2,1)} %slice.51), channel_id=1, source_target_pairs={{0,6},{2,0},{4,2},{6,4},{1,7},{3,1},{5,3},{7,5},{8,14},{10,8},{12,... | collective-permute-start | bytes 1769480 | tf_op jit(solution)/shard_map/ppermute | solution.py:30
  61.3 11.5 %collective-permute-done.8.refs_7_ = bf16[2,288,512]{2,1,0:T(8,128)(2,1)} collective-permute-done((bf16[2,288,512]{2,1,0:T(8,128)(2,1)S(1)}, bf16[2,288,512]{2,1,0:T(8,128)(2,1)}, u32[]{:S(2)}, u32[]{:S(2)}) %collective-permute-start.8) | collective-permute-done | bytes 589856 | tf_op jit(solution)/shard_map/ppermute | solution.py:30
  72.9 1.9 collective-permute-done.10.refs_7_
  75.1 2.2 %all-gather.2.cloned.1.call-done.refs_9_ = bf16[2304,1152]{1,0:T(8,128)(2,1)} async-done(((bf16[288,1152]{1,0:T(8,128)(2,1)}), bf16[2304,1152]{1,0:T(8,128)(2,1)}) %all-gather.2.cloned.1.call-update) | async-done | bytes 5308432 | tf_op jit(solution)/shard_map/all_gather | solution.py:227
  77.3 6.9 %shard_map.46 = (bf16[256,1152]{1,0:T(8,128)(2,1)S(1)}, bf16[256,1152]{1,0:T(8,128)(2,1)S(1)}) custom-call(s32[8]{0:T(128)S(1)} %stack.35.refs_0_, bf16[4,288,512]{2,1,0:T(8,128)(2,1)S(1)} %pad_maximum_fusion.refs_1_, bf16[4,288,512]{2,1,0:T(8,128)(2,1)S(1)} %collective-permute-done.3.refs_2_, bf16[4,288,512]{2,1,0:T(8,128)(2,1)S(1)} %collective-permute-done.4.refs_3_, ...), custom_call_target="tpu_custom_call" | custom-call | tf_op jit(solution)/shard_map/pallas_call | solution.py:55
  84.3 1.6 collective-permute-start.12
  86.4 11.1 %shard_map.47 = (bf16[512,1152]{1,0:T(8,128)(2,1)S(1)}, bf16[512,1152]{1,0:T(8,128)(2,1)S(1)}) custom-call(s32[8]{0:T(128)S(1)} %stack.35.refs_0_, bf16[4,288,512]{2,1,0:T(8,128)(2,1)S(1)} %pad_maximum_fusion.refs_1_, bf16[4,288,512]{2,1,0:T(8,128)(2,1)} %copy-done.5, bf16[4,288,512]{2,1,0:T(8,128)(2,1)} %copy-done.3, ...), custom_call_target="tpu_custom_call" | custom-call | tf_op jit(solution)/shard_map/pallas_call | solution.py:55
  97.5 1.9 collective-permute-done.12.from_down_ref
  105.8 8.3 %shard_map.49.refs_0_ = f32[512,1152]{1,0:T(8,128)} custom-call(s32[8]{0:T(128)S(1)} %stack.35.refs_0_, bf16[4,288,512]{2,1,0:T(8,128)(2,1)S(1)} %pad_maximum_fusion.refs_1_, bf16[4,288,512]{2,1,0:T(8,128)(2,1)S(1)} %copy-done.6, bf16[4,288,512]{2,1,0:T(8,128)(2,1)S(1)} %copy-done.4, bf16[4,288,512]{2,1,0:T(8,128)(2,1)} %collective-permute-done.5.refs_4_, ...), custom_call_target="tpu_custom_call" | custom-call | tf_op jit(solution)/shard_map/pallas_call | solution.py:55
  114.2 7.8 %collective-permute-done.20.refs_1_ = bf16[512,768]{1,0:T(8,128)(2,1)S(1)} collective-permute-done((bf16[512,768]{1,0:T(8,128)(2,1)S(1)}, bf16[512,768]{1,0:T(8,128)(2,1)S(1)}, u32[]{:S(2)}, u32[]{:S(2)}) %collective-permute-start.20) | collective-permute-done | bytes 786464 | tf_op jit(solution)/shard_map/ppermute | solution.py:30
  123.1 1.7 copy-done.1
  126.5 1.5 collective-permute-start.22
  127.9 2.7 %collective-permute-start.23 = (bf16[2,96,512]{2,1,0:T(8,128)(2,1)}, bf16[2,96,512]{2,1,0:T(8,128)(2,1)S(1)}, u32[]{:S(2)}, u32[]{:S(2)}) collective-permute-start(bf16[2,96,512]{2,1,0:T(8,128)(2,1)} %get-tuple-element.35), channel_id=1, source_target_pairs={{0,4},{2,6},{4,0},{6,2},{1,5},{3,7},{5,1},{7,3},{8,12},{10,14},{12... | collective-permute-start | bytes 589832 | tf_op jit(solution)/shard_map/ppermute | solution.py:30
  130.6 1.5 collective-permute-start.24
  132.9 10.2 %all-to-all-start = ((bf16[32,16,384]{2,1,0:T(8,128)(2,1)}), bf16[32,16,384]{2,1,0:T(8,128)(2,1)S(1)}, u32[]{:S(2)}, u32[]{:S(2)}) async-start(bf16[32,16,384]{2,1,0:T(8,128)(2,1)} %bitcast.10), calls=%async_computation | async-start | bytes 786432 | tf_op jit(solution)/shard_map/all_to_all | solution.py:215
  143.6 1.5 collective-permute-done.25.refs_4_
  146.2 8.1 %all-to-all-done = bf16[32,16,384]{2,1,0:T(8,128)(2,1)S(1)} async-done(((bf16[32,16,384]{2,1,0:T(8,128)(2,1)}), bf16[32,16,384]{2,1,0:T(8,128)(2,1)S(1)}, u32[]{:S(2)}, u32[]{:S(2)}) %all-to-all-start) | async-done | bytes 393248 | tf_op jit(solution)/shard_map/all_to_all | solution.py:215
  154.3 6.0 %all-to-all-start.1 = ((bf16[32,16,768]{2,1,0:T(8,128)(2,1)}), bf16[32,16,768]{2,1,0:T(8,128)(2,1)}, u32[]{:S(2)}, u32[]{:S(2)}) async-start(bf16[32,16,768]{2,1,0:T(8,128)(2,1)} %bitcast.12), calls=%async_computation.1 | async-start | bytes 1572864 | tf_op jit(solution)/shard_map/all_to_all | solution.py:215
  160.5 1.6 fusion.land_ref
  164.1 2.6 %collective-permute-start.17 = (bf16[2,48,512]{2,1,0:T(8,128)(2,1)S(1)}, bf16[2,48,512]{2,1,0:T(8,128)(2,1)S(1)}, u32[]{:S(2)}, u32[]{:S(2)}) collective-permute-start(bf16[2,48,512]{2,1,0:T(8,128)(2,1)S(1)} %get-tuple-element.29), channel_id=1, source_target_pairs={{0,4},{2,6},{4,0},{6,2},{1,5},{3,7},{5,1},{7,3},{8,12},{10,14},{12... | collective-permute-start | bytes 294920 | tf_op jit(solution)/shard_map/ppermute | solution.py:30
  168.8 1.6 collective-permute-done.17.refs_2_
  173.2 1.8 shard_map.53.begun_ref
  175.1 3.8 %all-to-all-done.1 = bf16[32,16,768]{2,1,0:T(8,128)(2,1)} async-done(((bf16[32,16,768]{2,1,0:T(8,128)(2,1)}), bf16[32,16,768]{2,1,0:T(8,128)(2,1)}, u32[]{:S(2)}, u32[]{:S(2)}) %all-to-all-start.1) | async-done | bytes 786464 | tf_op jit(solution)/shard_map/all_to_all | solution.py:215
  178.9 1.5 copy-done.7
  181.4 3.8 %shard_map.56 = bf16[512,1152]{1,0:T(8,128)(2,1)} custom-call(s32[512,2]{1,0:T(8,128)S(1)} %copy-done.11, f32[512,1152]{1,0:T(8,128)S(1)} %shard_map.53.begun_ref, bf16[512,512]{1,0:T(8,128)(2,1)S(1)} %copy-done.9, bf16[768,1152]{1,0:T(8,128)(2,1)S(1)} %copy-done.7, bf16[512,768]{1,0:T(8,128)(2,1)} %bitcast.13.received_ref), custom_call_target="tpu_custom_call" | custom-call | tf_op jit(solution)/shard_map/pallas_call | solution.py:204
  (97 shorter events, 27.1 us)
Async XLA Ops:
  6.5 70.8 %all-gather.2.cloned.1.call-start = ((), (), s32[]{:S(2)}) async-start(), calls=%async_computation.2 | async-start | bytes 5971968 | tf_op jit(solution)/shard_map/all_gather | solution.py:227
  9.4 11.5 %collective-permute-start = (bf16[1,288,512]{2,1,0:T(8,128)(2,1)S(1)}, bf16[1,288,512]{2,1,0:T(8,128)(2,1)S(1)}, u32[]{:S(2)}, u32[]{:S(2)}) collective-permute-start(bf16[1,288,512]{2,1,0:T(8,128)(2,1)S(1)} %get-tuple-element.42), channel_id=1, source_target_pairs={{0,16},{8,24},{16,0},{24,8},{1,17},{9,25},{17,1},{25,9},{2,18},{10... | collective-permute-start | bytes 884744 | tf_op jit(solution)/shard_map/ppermute | solution.py:30
  11.8 14.3 %collective-permute-start.1 = (bf16[1,288,512]{2,1,0:T(8,128)(2,1)S(1)}, bf16[1,288,512]{2,1,0:T(8,128)(2,1)S(1)}, u32[]{:S(2)}, u32[]{:S(2)}) collective-permute-start(bf16[1,288,512]{2,1,0:T(8,128)(2,1)S(1)} %get-tuple-element.41), channel_id=1, source_target_pairs={{0,24},{8,0},{16,8},{24,16},{1,25},{9,1},{17,9},{25,17},{2,26},{10... | collective-permute-start | bytes 884744 | tf_op jit(solution)/shard_map/ppermute | solution.py:30
  13.1 13.1 %collective-permute-start.2 = (bf16[1,288,512]{2,1,0:T(8,128)(2,1)S(1)}, bf16[1,288,512]{2,1,0:T(8,128)(2,1)S(1)}, u32[]{:S(2)}, u32[]{:S(2)}) collective-permute-start(bf16[1,288,512]{2,1,0:T(8,128)(2,1)S(1)} %get-tuple-element.40), channel_id=1, source_target_pairs={{0,8},{8,16},{16,24},{24,0},{1,9},{9,17},{17,25},{25,1},{2,10},{10... | collective-permute-start | bytes 884744 | tf_op jit(solution)/shard_map/ppermute | solution.py:30
  26.3 29.1 %collective-permute-start.4 = (bf16[4,288,512]{2,1,0:T(8,128)(2,1)S(1)}, bf16[4,288,512]{2,1,0:T(8,128)(2,1)S(1)}, u32[]{:S(2)}, u32[]{:S(2)}) collective-permute-start(bf16[4,288,512]{2,1,0:T(8,128)(2,1)S(1)} %pad_maximum_fusion.refs_1_), channel_id=1, source_target_pairs={{0,2},{2,4},{4,6},{6,0},{1,3},{3,5},{5,7},{7,1},{8,10},{10,12},{12... | collective-permute-start | bytes 3538952 | tf_op jit(solution)/shard_map/ppermute | solution.py:30
  27.9 27.7 %collective-permute-start.6 = (bf16[4,288,512]{2,1,0:T(8,128)(2,1)S(1)}, bf16[4,288,512]{2,1,0:T(8,128)(2,1)}, u32[]{:S(2)}, u32[]{:S(2)}) collective-permute-start(bf16[4,288,512]{2,1,0:T(8,128)(2,1)S(1)} %pad_maximum_fusion.refs_1_), channel_id=1, source_target_pairs={{0,6},{2,0},{4,2},{6,4},{1,7},{3,1},{5,3},{7,5},{8,14},{10,8},{12,... | collective-permute-start | bytes 3538952 | tf_op jit(solution)/shard_map/ppermute | solution.py:30
  29.7 45.1 %collective-permute-start.3 = (bf16[4,288,512]{2,1,0:T(8,128)(2,1)S(1)}, bf16[4,288,512]{2,1,0:T(8,128)(2,1)S(1)}, u32[]{:S(2)}, u32[]{:S(2)}) collective-permute-start(bf16[4,288,512]{2,1,0:T(8,128)(2,1)S(1)} %pad_maximum_fusion.refs_1_), channel_id=1, source_target_pairs={{0,1},{1,0},{2,3},{3,2},{4,5},{5,4},{6,7},{7,6},{8,9},{9,8},{10,11... | collective-permute-start | bytes 3538952 | tf_op jit(solution)/shard_map/ppermute | solution.py:30
  55.5 21.9 %copy-start.3 = (bf16[4,288,512]{2,1,0:T(8,128)(2,1)}, bf16[4,288,512]{2,1,0:T(8,128)(2,1)S(1)}, u32[]{:S(2)}) copy-start(bf16[4,288,512]{2,1,0:T(8,128)(2,1)S(1)} %collective-permute-done.4.refs_3_) | copy-start | bytes 3538948
  55.5 19.3 %collective-permute-start.5 = (bf16[4,288,512]{2,1,0:T(8,128)(2,1)S(1)}, bf16[4,288,512]{2,1,0:T(8,128)(2,1)}, u32[]{:S(2)}, u32[]{:S(2)}) collective-permute-start(bf16[4,288,512]{2,1,0:T(8,128)(2,1)S(1)} %collective-permute-done.4.refs_3_), channel_id=1, source_target_pairs={{0,1},{1,0},{2,3},{3,2},{4,5},{5,4},{6,7},{7,6},{8,9},{9,8},{10,11... | collective-permute-start | bytes 3538952 | tf_op jit(solution)/shard_map/ppermute | solution.py:30
  55.6 19.2 %collective-permute-start.7 = (bf16[4,288,512]{2,1,0:T(8,128)(2,1)}, bf16[4,288,512]{2,1,0:T(8,128)(2,1)}, u32[]{:S(2)}, u32[]{:S(2)}) collective-permute-start(bf16[4,288,512]{2,1,0:T(8,128)(2,1)} %collective-permute-done.6.refs_5_), channel_id=1, source_target_pairs={{0,1},{1,0},{2,3},{3,2},{4,5},{5,4},{6,7},{7,6},{8,9},{9,8},{10,11... | collective-permute-start | bytes 3538952 | tf_op jit(solution)/shard_map/ppermute | solution.py:30
  56.1 16.7 %collective-permute-start.8 = (bf16[2,288,512]{2,1,0:T(8,128)(2,1)S(1)}, bf16[2,288,512]{2,1,0:T(8,128)(2,1)}, u32[]{:S(2)}, u32[]{:S(2)}) collective-permute-start(bf16[2,288,512]{2,1,0:T(8,128)(2,1)S(1)} %slice.50), channel_id=1, source_target_pairs={{0,2},{2,4},{4,6},{6,0},{1,3},{3,5},{5,7},{7,1},{8,10},{10,12},{12... | collective-permute-start | bytes 1769480 | tf_op jit(solution)/shard_map/ppermute | solution.py:30
  59.0 15.8 %collective-permute-start.10 = (bf16[2,288,512]{2,1,0:T(8,128)(2,1)}, bf16[2,288,512]{2,1,0:T(8,128)(2,1)}, u32[]{:S(2)}, u32[]{:S(2)}) collective-permute-start(bf16[2,288,512]{2,1,0:T(8,128)(2,1)} %slice.51), channel_id=1, source_target_pairs={{0,6},{2,0},{4,2},{6,4},{1,7},{3,1},{5,3},{7,5},{8,14},{10,8},{12,... | collective-permute-start | bytes 1769480 | tf_op jit(solution)/shard_map/ppermute | solution.py:30
  72.8 2.3 %collective-permute-start.9 = (bf16[2,288,512]{2,1,0:T(8,128)(2,1)}, bf16[2,288,512]{2,1,0:T(8,128)(2,1)}, u32[]{:S(2)}, u32[]{:S(2)}) collective-permute-start(bf16[2,288,512]{2,1,0:T(8,128)(2,1)} %collective-permute-done.8.refs_7_), channel_id=1, source_target_pairs={{0,1},{1,0},{2,3},{3,2},{4,5},{5,4},{6,7},{7,6},{8,9},{9,8},{10,11... | collective-permute-start | bytes 1769480 | tf_op jit(solution)/shard_map/ppermute | solution.py:30
  74.8 11.6 %collective-permute-start.11 = (bf16[2,288,512]{2,1,0:T(8,128)(2,1)}, bf16[2,288,512]{2,1,0:T(8,128)(2,1)}, u32[]{:S(2)}, u32[]{:S(2)}) collective-permute-start(bf16[2,288,512]{2,1,0:T(8,128)(2,1)} %collective-permute-done.10.refs_7_), channel_id=1, source_target_pairs={{0,1},{1,0},{2,3},{3,2},{4,5},{5,4},{6,7},{7,6},{8,9},{9,8},{10,11... | collective-permute-start | bytes 1769480 | tf_op jit(solution)/shard_map/ppermute | solution.py:30
  74.8 9.5 %copy-start.5 = (bf16[4,288,512]{2,1,0:T(8,128)(2,1)}, bf16[4,288,512]{2,1,0:T(8,128)(2,1)S(1)}, u32[]{:S(2)}) copy-start(bf16[4,288,512]{2,1,0:T(8,128)(2,1)S(1)} %collective-permute-done.3.refs_2_) | copy-start | bytes 3538948
  84.3 15.1 %collective-permute-start.12 = (bf16[256,1152]{1,0:T(8,128)(2,1)S(1)}, bf16[256,1152]{1,0:T(8,128)(2,1)S(1)}, u32[]{:S(2)}, u32[]{:S(2)}) collective-permute-start(bf16[256,1152]{1,0:T(8,128)(2,1)S(1)} %get-tuple-element.21.refs_10_), channel_id=1, source_target_pairs={{0,8},{8,16},{16,24},{24,0},{1,9},{9,17},{17,25},{25,1},{2,10},{10... | collective-permute-start | bytes 1769480 | tf_op jit(solution)/shard_map/ppermute | solution.py:30
  85.8 14.8 %collective-permute-start.13 = (bf16[256,1152]{1,0:T(8,128)(2,1)S(1)}, bf16[256,1152]{1,0:T(8,128)(2,1)S(1)}, u32[]{:S(2)}, u32[]{:S(2)}) collective-permute-start(bf16[256,1152]{1,0:T(8,128)(2,1)S(1)} %get-tuple-element.24), channel_id=1, source_target_pairs={{0,24},{8,0},{16,8},{24,16},{1,25},{9,1},{17,9},{25,17},{2,26},{10... | collective-permute-start | bytes 1769480 | tf_op jit(solution)/shard_map/ppermute | solution.py:30
  101.4 20.6 %collective-permute-start.20 = (bf16[512,768]{1,0:T(8,128)(2,1)S(1)}, bf16[512,768]{1,0:T(8,128)(2,1)S(1)}, u32[]{:S(2)}, u32[]{:S(2)}) collective-permute-start(bf16[512,768]{1,0:T(8,128)(2,1)S(1)} %get-tuple-element.31), channel_id=1, source_target_pairs={{0,8},{8,16},{16,24},{24,0},{1,9},{9,17},{17,25},{25,1},{2,10},{10... | collective-permute-start | bytes 2359304 | tf_op jit(solution)/shard_map/ppermute | solution.py:30
  102.6 20.5 %collective-permute-start.21 = (bf16[512,768]{1,0:T(8,128)(2,1)S(1)}, bf16[512,768]{1,0:T(8,128)(2,1)S(1)}, u32[]{:S(2)}, u32[]{:S(2)}) collective-permute-start(bf16[512,768]{1,0:T(8,128)(2,1)S(1)} %get-tuple-element.32), channel_id=1, source_target_pairs={{0,24},{8,0},{16,8},{24,16},{1,25},{9,1},{17,9},{25,17},{2,26},{10... | collective-permute-start | bytes 2359304 | tf_op jit(solution)/shard_map/ppermute | solution.py:30
  103.5 28.6 %collective-permute-start.14 = (bf16[512,384]{1,0:T(8,128)(2,1)S(1)}, bf16[512,384]{1,0:T(8,128)(2,1)S(1)}, u32[]{:S(2)}, u32[]{:S(2)}) collective-permute-start(bf16[512,384]{1,0:T(8,128)(2,1)S(1)} %get-tuple-element.25.refs_10_), channel_id=1, source_target_pairs={{0,8},{8,16},{16,24},{24,0},{1,9},{9,17},{17,25},{25,1},{2,10},{10... | collective-permute-start | bytes 1179656 | tf_op jit(solution)/shard_map/ppermute | solution.py:30
  104.7 27.4 %collective-permute-start.15 = (bf16[512,384]{1,0:T(8,128)(2,1)S(1)}, bf16[512,384]{1,0:T(8,128)(2,1)S(1)}, u32[]{:S(2)}, u32[]{:S(2)}) collective-permute-start(bf16[512,384]{1,0:T(8,128)(2,1)S(1)} %get-tuple-element.26), channel_id=1, source_target_pairs={{0,24},{8,0},{16,8},{24,16},{1,25},{9,1},{17,9},{25,17},{2,26},{10... | collective-permute-start | bytes 1179656 | tf_op jit(solution)/shard_map/ppermute | solution.py:30
  126.5 16.7 %collective-permute-start.22 = (bf16[2,96,512]{2,1,0:T(8,128)(2,1)}, bf16[2,96,512]{2,1,0:T(8,128)(2,1)S(1)}, u32[]{:S(2)}, u32[]{:S(2)}) collective-permute-start(bf16[2,96,512]{2,1,0:T(8,128)(2,1)} %get-tuple-element.34), channel_id=1, source_target_pairs={{0,2},{2,4},{4,6},{6,0},{1,3},{3,5},{5,7},{7,1},{8,10},{10,12},{12... | collective-permute-start | bytes 589832 | tf_op jit(solution)/shard_map/ppermute | solution.py:30
  127.9 15.2 %collective-permute-start.23 = (bf16[2,96,512]{2,1,0:T(8,128)(2,1)}, bf16[2,96,512]{2,1,0:T(8,128)(2,1)S(1)}, u32[]{:S(2)}, u32[]{:S(2)}) collective-permute-start(bf16[2,96,512]{2,1,0:T(8,128)(2,1)} %get-tuple-element.35), channel_id=1, source_target_pairs={{0,4},{2,6},{4,0},{6,2},{1,5},{3,7},{5,1},{7,3},{8,12},{10,14},{12... | collective-permute-start | bytes 589832 | tf_op jit(solution)/shard_map/ppermute | solution.py:30
  130.6 12.6 %collective-permute-start.24 = (bf16[2,96,512]{2,1,0:T(8,128)(2,1)S(1)}, bf16[2,96,512]{2,1,0:T(8,128)(2,1)S(1)}, u32[]{:S(2)}, u32[]{:S(2)}) collective-permute-start(bf16[2,96,512]{2,1,0:T(8,128)(2,1)S(1)} %get-tuple-element.36), channel_id=1, source_target_pairs={{0,6},{2,0},{4,2},{6,4},{1,7},{3,1},{5,3},{7,5},{8,14},{10,8},{12,... | collective-permute-start | bytes 589832 | tf_op jit(solution)/shard_map/ppermute | solution.py:30
  132.9 10.4 %copy-start.13 = (s32[512]{0:T(512)S(1)}, s32[512]{0:T(512)}, u32[]{:S(2)}) copy-start(s32[512]{0:T(512)} %param.7) | copy-start | bytes 6148
  132.9 21.4 %all-to-all-start = ((bf16[32,16,384]{2,1,0:T(8,128)(2,1)}), bf16[32,16,384]{2,1,0:T(8,128)(2,1)S(1)}, u32[]{:S(2)}, u32[]{:S(2)}) async-start(bf16[32,16,384]{2,1,0:T(8,128)(2,1)} %bitcast.10), calls=%async_computation | async-start | bytes 786432 | tf_op jit(solution)/shard_map/all_to_all | solution.py:215
  143.3 1.8 collective-permute-start.25
  154.3 24.5 %all-to-all-start.1 = ((bf16[32,16,768]{2,1,0:T(8,128)(2,1)}), bf16[32,16,768]{2,1,0:T(8,128)(2,1)}, u32[]{:S(2)}, u32[]{:S(2)}) async-start(bf16[32,16,768]{2,1,0:T(8,128)(2,1)} %bitcast.12), calls=%async_computation.1 | async-start | bytes 1572864 | tf_op jit(solution)/shard_map/all_to_all | solution.py:215
  162.9 5.9 %collective-permute-start.16 = (bf16[2,48,512]{2,1,0:T(8,128)(2,1)S(1)}, bf16[2,48,512]{2,1,0:T(8,128)(2,1)S(1)}, u32[]{:S(2)}, u32[]{:S(2)}) collective-permute-start(bf16[2,48,512]{2,1,0:T(8,128)(2,1)S(1)} %get-tuple-element.28), channel_id=1, source_target_pairs={{0,2},{2,4},{4,6},{6,0},{1,3},{3,5},{5,7},{7,1},{8,10},{10,12},{12... | collective-permute-start | bytes 294920 | tf_op jit(solution)/shard_map/ppermute | solution.py:30
  164.1 6.3 %collective-permute-start.17 = (bf16[2,48,512]{2,1,0:T(8,128)(2,1)S(1)}, bf16[2,48,512]{2,1,0:T(8,128)(2,1)S(1)}, u32[]{:S(2)}, u32[]{:S(2)}) collective-permute-start(bf16[2,48,512]{2,1,0:T(8,128)(2,1)S(1)} %get-tuple-element.29), channel_id=1, source_target_pairs={{0,4},{2,6},{4,0},{6,2},{1,5},{3,7},{5,1},{7,3},{8,12},{10,14},{12... | collective-permute-start | bytes 294920 | tf_op jit(solution)/shard_map/ppermute | solution.py:30
  166.8 4.6 %collective-permute-start.18 = (bf16[2,48,512]{2,1,0:T(8,128)(2,1)S(1)}, bf16[2,48,512]{2,1,0:T(8,128)(2,1)S(1)}, u32[]{:S(2)}, u32[]{:S(2)}) collective-permute-start(bf16[2,48,512]{2,1,0:T(8,128)(2,1)S(1)} %get-tuple-element.30), channel_id=1, source_target_pairs={{0,6},{2,0},{4,2},{6,4},{1,7},{3,1},{5,3},{7,5},{8,14},{10,8},{12,... | collective-permute-start | bytes 294920 | tf_op jit(solution)/shard_map/ppermute | solution.py:30
  171.4 1.8 collective-permute-start.19
  (11 other events, 33.6 us)
Sparse Core Ops, SparseCore 0:
  9.1 68.1 all-gather.1
